TPU v7x, 32 devices: a whole 2x2x4 slice. The times are simulated.
32 devices in a mesh: grp: 4 (over z), mod: 8 (over y, x, core).
Axes of the slice: x: 2, y: 2, z: 4, core: 2. Of those that a mesh axis runs over, the one named last changes fastest.
Arguments:
- tokens: bfloat16 [64, 64, 8, 128], P(('grp', 'mod')), may hold values from -3 to 3
- lengths: int32 [64], P(('grp', 'mod')), may hold values from 1 to 64, 2048 in all
- module_order: int32 [8], replicated, may hold values from 0 to 7, each once
Outputs:
- preconditioned: float32 [8, 64, 4096], P('mod', 'grp')
Inputs may be any that keep to these rules, and one draw needn't show every extreme that they name: `lengths`: each example's live tokens are its first slots; some example has exactly 64. `module_order`: each module appears exactly once.
All inputs are finite; a program needn't handle non-finite values. No bound on the sum of `lengths` on one device may be relied on, other than what follows from the above.
Results may differ from a plain program's by a relative error of at most 0.0068.
Values may be sent and summed in bfloat16 or wider, within the bound.
No kernel may reach another device: no remote copies, remote signals or barrier semaphores. Data moves between devices by JAX's collectives and lax.ppermute only.
A program may use at most 64 MiB of HBM per device.

v0:
```python
import jax
import jax.numpy as jnp
from jax import lax
from jax.sharding import PartitionSpec as P

ITERS = 3


def partner(value, axis, bit):
    mask = 2**bit
    pairs = [(source, source ^ mask) for source in range(lax.axis_size(axis))]
    return lax.ppermute(value, axis, pairs)


def start_basis(row_count, col_count):
    row_index = jnp.arange(row_count, dtype=jnp.float32)[:, None] + 0.5
    col_index = jnp.arange(col_count, dtype=jnp.float32)[None, :] + 0.5
    return jnp.cos(jnp.pi * row_index * col_index / row_count)


def orthonormal(matrix):
    for repeat in range(2):
        cross_gram = jnp.dot(matrix.T, matrix, precision=lax.Precision.HIGHEST)
        factor = jnp.linalg.cholesky(cross_gram)
        matrix = jax.scipy.linalg.solve_triangular(factor, matrix.T, lower=True).T
    return matrix


def merge_pair(lower_sketch, upper_sketch):
    stacked = jnp.concatenate([lower_sketch, upper_sketch], axis=0)
    kernel = jnp.dot(stacked, stacked.T, precision=lax.Precision.HIGHEST)
    current = start_basis(stacked.shape[0], lower_sketch.shape[0])
    for repeat in range(ITERS):
        current = orthonormal(jnp.dot(kernel, current, precision=lax.Precision.HIGHEST))
    return jnp.dot(current.T, stacked, precision=lax.Precision.HIGHEST)


def precondition(group_rows, sketch):
    sketch_rows = sketch.shape[0]
    damping = 0.1 * jnp.sum(sketch * sketch) / sketch_rows + 1e-06
    capacitance = jnp.dot(sketch, sketch.T, precision=lax.Precision.HIGHEST) + damping * jnp.eye(
        sketch_rows, dtype=jnp.float32
    )
    projected = jnp.dot(group_rows, sketch.T, precision=lax.Precision.HIGHEST)
    factor = jnp.linalg.cholesky(capacitance)
    middle = jax.scipy.linalg.solve_triangular(factor, projected.T, lower=True)
    weights = jax.scipy.linalg.solve_triangular(factor, middle, lower=True, trans=1).T
    return group_rows - jnp.dot(weights, sketch, precision=lax.Precision.HIGHEST)


def local_features(token_block, live_counts):
    example_count, token_slots, module_count, full_width = token_block.shape
    half_width = full_width // 2
    live_mask = jnp.arange(token_slots, dtype=jnp.int32)[None, :] < live_counts[:, None]
    grad_side = jnp.where(
        live_mask[:, :, None, None],
        token_block[:, :, :, half_width:],
        jnp.zeros((), token_block.dtype),
    )
    input_side = token_block[:, :, :, :half_width]
    outer = jnp.einsum("etmo,etmi->meoi", grad_side, input_side, preferred_element_type=jnp.float32)
    return outer.reshape(module_count, example_count, half_width * half_width).astype(jnp.bfloat16)


def per_device(tokens, lengths, module_order):
    features = local_features(tokens, lengths)
    ordered = jnp.take(features, module_order, axis=0)
    group_rows = lax.all_to_all(ordered, "mod", split_axis=0, concat_axis=1, tiled=True)
    leaves = group_rows.astype(jnp.float32)
    merge_all = jax.vmap(merge_pair)
    levels = lax.axis_size("grp").bit_length() - 1
    position = lax.axis_index("grp")
    sketch = leaves
    for height in range(levels):
        sister = partner(sketch, "grp", height)
        upper_side = position // 2**height % 2 == 1
        lower_part = jnp.where(upper_side, sister, sketch)
        upper_part = jnp.where(upper_side, sketch, sister)
        sketch = merge_all(lower_part, upper_part)
    return jax.vmap(precondition)(leaves, sketch)


def solution(mesh):
    return jax.shard_map(
        per_device,
        mesh=mesh,
        in_specs=(P(("grp", "mod"), None, None, None), P(("grp", "mod")), P()),
        out_specs=P("mod", "grp", None),
        check_vma=False,
    )
```

profile of v0, /device:TPU:0, one launch (start us, length us, event | category | flops | bytes accessed | tf_op | source)
XLA Modules:
  0.0 100.7 jit_solution(14928958920821151999)
XLA Ops:
  1.5 1.3 %slice_select_fusion = (bf16[2,64,8,64]{3,2,1,0:T(8,128)(2,1)S(1)}, bf16[2,64,8,64]{3,2,1,0:T(8,128)(2,1)S(1)}) fusion(bf16[2,64,8,128]{3,2,1,0:T(8,128)(2,1)} %param.6, pred[2,64]{1,0:T(4,128)(4,1)S(1)} %iota_compare_fusion.3), kind=kLoop, calls=%fused_computation.15 | loop fusion | flops 65536 | bytes 524416 | tf_op jit(solution)/shard_map/jit(_where)/select_n | solution.py:55
  4.3 10.5 %all_to_all.12 = bf16[8,2,4096]{2,1,0:T(2,128)(2,1)S(1)} all-to-all(bf16[8,2,4096]{2,1,0:T(2,128)(2,1)S(1)} %broadcast_select_fusion), channel_id=1, replica_groups=mesh['grp'=4,'mod'=8] {'mod'}, dimensions={0} | all-to-all | bytes 262144 | tf_op jit(solution)/shard_map/all_to_all | solution.py:68
  14.8 1.6 %collective-permute-start = (f32[1,16,4096]{2,1,0:T(8,128)S(1)}, f32[1,16,4096]{2,1,0:T(8,128)S(1)}, u32[]{:S(2)}, u32[]{:S(2)}) collective-permute-start(f32[1,16,4096]{2,1,0:T(8,128)S(1)} %reshape.327), channel_id=1, source_target_pairs={{0,8},{8,0},{16,24},{24,16},{1,9},{9,1},{17,25},{25,17},{2,10},{10... | collective-permute-start | bytes 786440 | tf_op jit(solution)/shard_map/ppermute | solution.py:12
  16.5 6.3 %collective-permute-done = f32[1,16,4096]{2,1,0:T(8,128)S(1)} collective-permute-done((f32[1,16,4096]{2,1,0:T(8,128)S(1)}, f32[1,16,4096]{2,1,0:T(8,128)S(1)}, u32[]{:S(2)}, u32[]{:S(2)}) %collective-permute-start) | collective-permute-done | bytes 262176 | tf_op jit(solution)/shard_map/ppermute | solution.py:12
  23.9 1.5 %custom-call.37 = f32[1,16,16]{2,1,0:T(8,128)S(1)} custom-call(f32[1,16,16]{2,1,0:T(8,128)S(1)} %fusion.45), custom_call_target="Cholesky" | custom-call | tf_op jit(solution)/shard_map/vmap(jit(cholesky))/cholesky | solution.py:24
  26.7 1.2 %custom-call.38 = f32[1,1,16,16]{2,3,1,0:T(8,128)S(1)} custom-call(f32[1,1,16,16]{3,2,1,0:T(8,128)S(1)} %fusion.8), custom_call_target="InvertDiagBlocksLowerTriangular" | custom-call | tf_op jit(solution)/shard_map/vmap(jit(_solve_triangular))/triangular_solve | solution.py:25
  28.4 1.5 %custom-call.39 = f32[1,16,16]{2,1,0:T(8,128)S(1)} custom-call(f32[1,16,16]{2,1,0:T(8,128)S(1)} %fusion.42), custom_call_target="Cholesky" | custom-call | tf_op jit(solution)/shard_map/vmap(jit(cholesky))/cholesky | solution.py:24
  31.2 1.2 %custom-call.40 = f32[1,1,16,16]{2,3,1,0:T(8,128)S(1)} custom-call(f32[1,1,16,16]{3,2,1,0:T(8,128)S(1)} %fusion.9), custom_call_target="InvertDiagBlocksLowerTriangular" | custom-call | tf_op jit(solution)/shard_map/vmap(jit(_solve_triangular))/triangular_solve | solution.py:25
  33.0 1.5 %custom-call.41 = f32[1,16,16]{2,1,0:T(8,128)S(1)} custom-call(f32[1,16,16]{2,1,0:T(8,128)S(1)} %fusion.41), custom_call_target="Cholesky" | custom-call | tf_op jit(solution)/shard_map/vmap(jit(cholesky))/cholesky | solution.py:24
  35.8 1.2 %custom-call.42 = f32[1,1,16,16]{2,3,1,0:T(8,128)S(1)} custom-call(f32[1,1,16,16]{3,2,1,0:T(8,128)S(1)} %fusion.10), custom_call_target="InvertDiagBlocksLowerTriangular" | custom-call | tf_op jit(solution)/shard_map/vmap(jit(_solve_triangular))/triangular_solve | solution.py:25
  37.4 1.5 %custom-call.43 = f32[1,16,16]{2,1,0:T(8,128)S(1)} custom-call(f32[1,16,16]{2,1,0:T(8,128)S(1)} %fusion.38), custom_call_target="Cholesky" | custom-call | tf_op jit(solution)/shard_map/vmap(jit(cholesky))/cholesky | solution.py:24
  40.2 1.2 %custom-call.44 = f32[1,1,16,16]{2,3,1,0:T(8,128)S(1)} custom-call(f32[1,1,16,16]{3,2,1,0:T(8,128)S(1)} %fusion.11), custom_call_target="InvertDiagBlocksLowerTriangular" | custom-call | tf_op jit(solution)/shard_map/vmap(jit(_solve_triangular))/triangular_solve | solution.py:25
  42.1 1.5 %custom-call.45 = f32[1,16,16]{2,1,0:T(8,128)S(1)} custom-call(f32[1,16,16]{2,1,0:T(8,128)S(1)} %fusion.37), custom_call_target="Cholesky" | custom-call | tf_op jit(solution)/shard_map/vmap(jit(cholesky))/cholesky | solution.py:24
  46.5 1.5 %custom-call.47 = f32[1,16,16]{2,1,0:T(8,128)S(1)} custom-call(f32[1,16,16]{2,1,0:T(8,128)S(1)} %fusion.34), custom_call_target="Cholesky" | custom-call | tf_op jit(solution)/shard_map/vmap(jit(cholesky))/cholesky | solution.py:24
  51.2 2.7 %collective-permute-start.1 = (f32[1,16,4096]{2,1,0:T(8,128)S(1)}, f32[1,16,4096]{2,1,0:T(8,128)S(1)}, u32[]{:S(2)}, u32[]{:S(2)}) collective-permute-start(f32[1,16,4096]{2,1,0:T(8,128)S(1)} %convolution_bitcast_fusion), channel_id=1, source_target_pairs={{0,16},{8,24},{16,0},{24,8},{1,17},{9,25},{17,1},{25,9},{2,18},{10... | collective-permute-start | bytes 786440 | tf_op jit(solution)/shard_map/ppermute | solution.py:12
  53.9 10.8 %collective-permute-done.1 = f32[1,16,4096]{2,1,0:T(8,128)S(1)} collective-permute-done((f32[1,16,4096]{2,1,0:T(8,128)S(1)}, f32[1,16,4096]{2,1,0:T(8,128)S(1)}, u32[]{:S(2)}, u32[]{:S(2)}) %collective-permute-start.1) | collective-permute-done | bytes 262176 | tf_op jit(solution)/shard_map/ppermute | solution.py:12
  65.8 1.5 %custom-call.49 = f32[1,16,16]{2,1,0:T(8,128)S(1)} custom-call(f32[1,16,16]{2,1,0:T(8,128)S(1)} %fusion.33), custom_call_target="Cholesky" | custom-call | tf_op jit(solution)/shard_map/vmap(jit(cholesky))/cholesky | solution.py:24
  70.3 1.5 %custom-call.51 = f32[1,16,16]{2,1,0:T(8,128)S(1)} custom-call(f32[1,16,16]{2,1,0:T(8,128)S(1)} %fusion.30), custom_call_target="Cholesky" | custom-call | tf_op jit(solution)/shard_map/vmap(jit(cholesky))/cholesky | solution.py:24
  74.9 1.5 %custom-call.53 = f32[1,16,16]{2,1,0:T(8,128)S(1)} custom-call(f32[1,16,16]{2,1,0:T(8,128)S(1)} %fusion.29), custom_call_target="Cholesky" | custom-call | tf_op jit(solution)/shard_map/vmap(jit(cholesky))/cholesky | solution.py:24
  79.4 1.5 %custom-call.55 = f32[1,16,16]{2,1,0:T(8,128)S(1)} custom-call(f32[1,16,16]{2,1,0:T(8,128)S(1)} %fusion.26), custom_call_target="Cholesky" | custom-call | tf_op jit(solution)/shard_map/vmap(jit(cholesky))/cholesky | solution.py:24
  82.2 1.2 %custom-call.56 = f32[1,1,16,16]{2,3,1,0:T(8,128)S(1)} custom-call(f32[1,1,16,16]{3,2,1,0:T(8,128)S(1)} %fusion.17), custom_call_target="InvertDiagBlocksLowerTriangular" | custom-call | tf_op jit(solution)/shard_map/vmap(jit(_solve_triangular))/triangular_solve | solution.py:25
  84.0 1.5 %custom-call.57 = f32[1,16,16]{2,1,0:T(8,128)S(1)} custom-call(f32[1,16,16]{2,1,0:T(8,128)S(1)} %fusion.25), custom_call_target="Cholesky" | custom-call | tf_op jit(solution)/shard_map/vmap(jit(cholesky))/cholesky | solution.py:24
  88.5 1.5 %custom-call.59 = f32[1,16,16]{2,1,0:T(8,128)S(1)} custom-call(f32[1,16,16]{2,1,0:T(8,128)S(1)} %fusion.22), custom_call_target="Cholesky" | custom-call | tf_op jit(solution)/shard_map/vmap(jit(cholesky))/cholesky | solution.py:24
  94.9 1.5 %custom-call.61 = f32[1,16,16]{2,1,0:T(8,128)S(1)} custom-call(f32[1,16,16]{2,1,0:T(8,128)S(1)} %fusion.21), custom_call_target="Cholesky" | custom-call | tf_op jit(solution)/shard_map/vmap(jit(cholesky))/cholesky | solution.py:45
  (130 shorter events, 41.4 us)
Async XLA Ops:
  0.0 0.7 copy-start
  0.7 0.7 copy-start.1
  14.8 7.9 %collective-permute-start = (f32[1,16,4096]{2,1,0:T(8,128)S(1)}, f32[1,16,4096]{2,1,0:T(8,128)S(1)}, u32[]{:S(2)}, u32[]{:S(2)}) collective-permute-start(f32[1,16,4096]{2,1,0:T(8,128)S(1)} %reshape.327), channel_id=1, source_target_pairs={{0,8},{8,0},{16,24},{24,16},{1,9},{9,1},{17,25},{25,17},{2,10},{10... | collective-permute-start | bytes 786440 | tf_op jit(solution)/shard_map/ppermute | solution.py:12
  51.2 13.5 %collective-permute-start.1 = (f32[1,16,4096]{2,1,0:T(8,128)S(1)}, f32[1,16,4096]{2,1,0:T(8,128)S(1)}, u32[]{:S(2)}, u32[]{:S(2)}) collective-permute-start(f32[1,16,4096]{2,1,0:T(8,128)S(1)} %convolution_bitcast_fusion), channel_id=1, source_target_pairs={{0,16},{8,24},{16,0},{24,8},{1,17},{9,25},{17,1},{25,9},{2,18},{10... | collective-permute-start | bytes 786440 | tf_op jit(solution)/shard_map/ppermute | solution.py:12
where the time goes:
time: 101 us
  other arithmetic  54.8 us (54%)
  waiting for transfers between devices  17.1 us (17%)
  blocking collectives  10.5 us (10%)
  matrix products  10.4 us (10%)
  starting transfers between devices  4.3 us (4%)
  local copies, waits for them, and re-layouts  2.73 us (3%)
    another operation x36, other arithmetic, orthonormal(): factor = jnp.linalg.cholesky(cross_gram)  25.7 us
    another operation x24, other arithmetic, orthonormal(): matrix = jax.scipy.linalg.solve_triangular(factor, matrix.T, lower=True).T  22.5 us
    ppermute x2, waiting for transfers between devices, partner(): return lax.ppermute(value, axis, pairs)  17.1 us
    all_to_all x1, blocking collectives, per_device(): lax.all_to_all(ordered, 'mod', split_axis=0, concat_axis=1, tiled=True)  10.5 us
    ppermute x2, starting transfers between devices, partner(): return lax.ppermute(value, axis, pairs)  4.3 us
    another operation x12, matrix products, orthonormal(): matrix = jax.scipy.linalg.solve_triangular(factor, matrix.T, lower=True).T  2.44 us
    another operation x3, other arithmetic, precondition(): factor = jnp.linalg.cholesky(capacitance)  2.14 us
  transfers between devices with their start and end apart: 2, of which 2 were waited for; matrix products, arithmetic and copies ran while one was open for 0% of the time, Pallas kernels for 0%

commit v1 on v0

v1 whole, which is shorter than its diff:
```python
import functools

import jax
import jax.numpy as jnp
import numpy as np
from jax import lax
from jax.experimental import pallas as pl
from jax.experimental.pallas import tpu as pltpu
from jax.sharding import PartitionSpec as P

ITERS = 3
HI = lax.Precision.HIGHEST


def partner(value, axis, bit):
    mask = 2**bit
    return xor_send(value, axis, mask)


def xor_send(value, axis, mask):
    pairs = [(source, source ^ mask) for source in range(lax.axis_size(axis))]
    return lax.ppermute(value, axis, pairs)


def start_basis(row_count, col_count):
    row_index = np.arange(row_count, dtype=np.float64)[:, None] + 0.5
    col_index = np.arange(col_count, dtype=np.float64)[None, :] + 0.5
    return np.cos(np.pi * row_index * col_index / row_count).astype(np.float32)


def orthonormal(matrix):
    for repeat in range(2):
        cross_gram = jnp.dot(matrix.T, matrix, precision=HI)
        factor = jnp.linalg.cholesky(cross_gram)
        matrix = jax.scipy.linalg.solve_triangular(factor, matrix.T, lower=True).T
    return matrix


def merge_pair(lower_sketch, upper_sketch):
    stacked = jnp.concatenate([lower_sketch, upper_sketch], axis=0)
    kernel = jnp.dot(stacked, stacked.T, precision=HI)
    current = start_basis(stacked.shape[0], lower_sketch.shape[0])
    for repeat in range(ITERS):
        current = orthonormal(jnp.dot(kernel, current, precision=HI))
    return jnp.dot(current.T, stacked, precision=HI)


def precondition(group_rows, sketch):
    sketch_rows = sketch.shape[0]
    damping = 0.1 * jnp.sum(sketch * sketch) / sketch_rows + 1e-06
    capacitance = jnp.dot(sketch, sketch.T, precision=HI) + damping * jnp.eye(sketch_rows, dtype=jnp.float32)
    projected = jnp.dot(group_rows, sketch.T, precision=HI)
    factor = jnp.linalg.cholesky(capacitance)
    middle = jax.scipy.linalg.solve_triangular(factor, projected.T, lower=True)
    weights = jax.scipy.linalg.solve_triangular(factor, middle, lower=True, trans=1).T
    return group_rows - jnp.dot(weights, sketch, precision=HI)


def sketch_tree(features, module_order):
    ordered = jnp.take(features, module_order, axis=0)
    group_rows = lax.all_to_all(ordered, "mod", split_axis=0, concat_axis=1, tiled=True)
    leaves = group_rows.astype(jnp.float32)
    merge_all = jax.vmap(merge_pair)
    levels = lax.axis_size("grp").bit_length() - 1
    position = lax.axis_index("grp")
    sketch = leaves
    for height in range(levels):
        sister = partner(sketch, "grp", height)
        upper_side = position // 2**height % 2 == 1
        lower_part = jnp.where(upper_side, sister, sketch)
        upper_part = jnp.where(upper_side, sketch, sister)
        sketch = merge_all(lower_part, upper_part)
    return jax.vmap(precondition)(leaves, sketch)


def dot_nt(a, b):
    return lax.dot_general(a, b, (((1,), (1,)), ((), ())), precision=HI, preferred_element_type=jnp.float32)


def dot_nn(a, b):
    return jnp.dot(a, b, precision=HI, preferred_element_type=jnp.float32)


def spread_columns(gram, first, count, width):
    columns = []
    for j in range(count):
        column = gram[first : first + count, first + j : first + j + 1]
        blocks = {b: jnp.broadcast_to(column[8 * b : 8 * b + 8], (8, width)) for b in range(j // 8, count // 8)}
        columns.append(blocks)
    return columns


def eliminate(columns, rhs):
    count = len(columns)
    width = rhs.shape[1]
    parts = [rhs[8 * b : 8 * b + 8] for b in range(count // 8)]
    row = lax.broadcasted_iota(jnp.int32, (8, width), 0)
    diag = [jnp.ones((8, width), jnp.float32) for _ in parts]
    for p in range(count):
        home, at = divmod(p, 8)
        pivot_column = columns[p]
        pivot = pivot_column[home][at : at + 1]
        diag[home] = jnp.where(row == at, pivot, diag[home])
        if p == count - 1:
            break
        inverse = 1.0 / pivot
        factor = {}
        for b in pivot_column:
            scaled = pivot_column[b] * inverse
            factor[b] = jnp.where(row > at, scaled, 0.0) if b == home else scaled
        for j in range(p + 1, count):
            along = pivot_column[j // 8][j % 8 : j % 8 + 1]
            columns[j] = {b: block - factor[b] * along for b, block in columns[j].items()}
        pivot_row = parts[home][at : at + 1]
        for b in factor:
            parts[b] = parts[b] - factor[b] * pivot_row
    return jnp.concatenate([part * lax.rsqrt(d) for part, d in zip(parts, diag)], axis=0)


def orthogonal_iteration(start, kernel, problems):
    rows = start.shape[0] // problems
    moved = dot_nn(start, kernel)
    for step in range(ITERS + 1):
        gram = dot_nt(moved, moved)
        onward = dot_nn(moved, kernel) if step < ITERS - 1 else moved
        done = []
        for k in range(problems):
            columns = spread_columns(gram, k * rows, rows, onward.shape[1])
            done.append(eliminate(columns, onward[k * rows : (k + 1) * rows]))
        moved = jnp.concatenate(done, axis=0)
    return moved


def combine_kernel(rows, near_ref, a_ref, b_ref, c_ref, start_ref, pair_ref, leaf_ref, out_ref):
    gram = (near_ref[...] + a_ref[...]) + (b_ref[...] + c_ref[...])
    count = gram.shape[0]
    half = count // 2
    r = lax.broadcasted_iota(jnp.int32, gram.shape, 0)
    c = lax.broadcasted_iota(jnp.int32, gram.shape, 1)
    own_pair = jnp.where((r < half) == (c < half), gram, 0.0)
    first = orthogonal_iteration(pair_ref[...], own_pair, 2)
    reached = dot_nn(first, gram)
    kernel = dot_nt(reached, first)
    second = orthogonal_iteration(start_ref[...], kernel, 1)
    weights = dot_nn(second, first)
    projected = dot_nn(second, reached)
    capacitance = dot_nt(projected, weights)
    columns = spread_columns(capacitance, 0, rows, 2 * count)
    total = sum(columns[j][j // 8][j % 8 : j % 8 + 1] for j in range(rows))
    damping = 0.1 * total / rows + 1e-06
    row = lax.broadcasted_iota(jnp.int32, (8, 2 * count), 0)
    for j in range(rows):
        columns[j][j // 8] = columns[j][j // 8] + jnp.where(row == j % 8, damping, 0.0)
    solved = eliminate(columns, jnp.concatenate([projected, weights], axis=1))
    change = lax.dot_general(
        solved[:, :count], solved[:, count:], (((0,), (0,)), ((), ())), precision=HI, preferred_element_type=jnp.float32
    )
    top = change.astype(jnp.bfloat16)
    rest = (change - top.astype(jnp.float32)).astype(jnp.bfloat16)
    leaf = leaf_ref[...]
    moved = jnp.dot(top, leaf, preferred_element_type=jnp.float32) + jnp.dot(rest, leaf, preferred_element_type=jnp.float32)
    out_ref[...] = (leaf.astype(jnp.float32) - moved).astype(out_ref.dtype)


def gram_route(features, module_order):
    groups, owners = lax.axis_size("grp"), lax.axis_size("mod")
    modules, own, width = features.shape
    rows = owners * own
    count = groups * rows
    ordered = jnp.take(features, module_order, axis=0)
    pieces = ordered.reshape(modules, own, groups, width // groups).transpose(2, 0, 1, 3)
    pieces = pieces.reshape(groups * modules, own, width // groups)
    leaf = lax.all_to_all(pieces, ("grp", "mod"), split_axis=0, concat_axis=0, tiled=True)
    leaf = leaf.reshape(count, width // groups)
    gram = lax.dot_general(leaf, leaf, (((1,), (1,)), ((), ())), preferred_element_type=jnp.float32)
    others = [xor_send(gram, "grp", mask) for mask in range(1, groups)]
    start = start_basis(2 * rows, rows).T
    pair = np.zeros((2 * rows, 4 * rows), np.float32)
    pair[:rows, : 2 * rows] = start
    pair[rows:, 2 * rows :] = start
    out = pl.pallas_call(
        functools.partial(combine_kernel, rows),
        out_shape=jax.ShapeDtypeStruct(leaf.shape, jnp.bfloat16),
        compiler_params=pltpu.CompilerParams(vmem_limit_bytes=32 * 1024 * 1024),
    )(gram, *others, jnp.asarray(start), jnp.asarray(pair), leaf)
    blocks = out.reshape(groups, rows, width // groups)
    me = lax.axis_index("grp")
    received = [lax.dynamic_index_in_dim(blocks, me, 0, keepdims=False)]
    for mask in range(1, groups):
        mine = lax.dynamic_index_in_dim(blocks, me ^ mask, 0, keepdims=False)
        received.append(xor_send(mine, "grp", mask))
    received = jnp.stack(received)
    chunks = [lax.dynamic_index_in_dim(received, me ^ g, 0, keepdims=False) for g in range(groups)]
    return jnp.concatenate(chunks, axis=1).astype(jnp.float32)[None]


def local_features(token_block, live_counts):
    example_count, token_slots, module_count, full_width = token_block.shape
    half_width = full_width // 2
    live_mask = jnp.arange(token_slots, dtype=jnp.int32)[None, :] < live_counts[:, None]
    grad_side = jnp.where(
        live_mask[:, :, None, None],
        token_block[:, :, :, half_width:],
        jnp.zeros((), token_block.dtype),
    )
    input_side = token_block[:, :, :, :half_width]
    outer = jnp.einsum("etmo,etmi->meoi", grad_side, input_side, preferred_element_type=jnp.float32)
    return outer.reshape(module_count, example_count, half_width * half_width).astype(jnp.bfloat16)


def per_device(tokens, lengths, module_order):
    features = local_features(tokens, lengths)
    groups, owners = lax.axis_size("grp"), lax.axis_size("mod")
    rows = owners * features.shape[1]
    if groups == 4 and rows == 16 and owners == features.shape[0]:
        return gram_route(features, module_order)
    return sketch_tree(features, module_order)


def solution(mesh):
    return jax.shard_map(
        per_device,
        mesh=mesh,
        in_specs=(P(("grp", "mod"), None, None, None), P(("grp", "mod")), P()),
        out_specs=P("mod", "grp", None),
        check_vma=False,
    )
```

time: 101 us -> 42.5 us (0.42)
  other arithmetic: 54.8 us -> 3.04 us
  matrix products: 10.4 us -> 0.44 us
  waiting for transfers between devices: 17.1 us -> 7.59 us
  Pallas kernels: 0 us -> 5.13 us
  blocking collectives: 10.5 us -> 15.3 us
  starting transfers between devices: 4.3 us -> 8.9 us
    another operation x65 -> x1, other arithmetic: 52.3 us -> 0.02 us  [gram_route(): received = jnp.stack(received)]
    ppermute x2 -> x6, waiting for transfers between devices: 17.1 us -> 7.59 us  [xor_send(): return lax.ppermute(value, axis, pairs)]
    dot_general x25 -> x1, matrix products: 7.4 us -> 0.17 us  [gram_route(): lax.dot_general(leaf, leaf, (((1,), (1,)), ((), ())), preferred_element_t...]
    pallas_call x0 -> x1, Pallas kernels: none -> 5.13 us  [gram_route(): pl.pallas_call(functools.partial(combine_kernel, rows), out_shape=jax.Sha...]
    all_to_all x1, blocking collectives: 10.5 us -> 15.3 us  [gram_route(): lax.all_to_all(pieces, ('grp', 'mod'), split_axis=0, concat_axis=0, tiled...]
    ppermute x2 -> x6, starting transfers between devices: 4.3 us -> 8.9 us  [xor_send(): return lax.ppermute(value, axis, pairs)]
    another operation x14 -> x0, matrix products: 2.78 us -> none  [the longest x12 2.44 us: orthonormal(): matrix = jax.scipy.linalg.solve_triangular(factor, matrix.T, lower=True).T]
  transfers between devices with their start and end apart: 2 -> 6, of which waited for: 2 -> 4; matrix products, arithmetic and copies ran while one was open for 0% -> 0% of each run, Pallas kernels for 0% -> 0%
where the time goes in v1:
time: 42.5 us; the launch traced here: 42.3 us
  blocking collectives  15.3 us (36%)
  starting transfers between devices  8.9 us (21%)
  waiting for transfers between devices  7.59 us (18%)
  Pallas kernels  5.13 us (12%)
  other arithmetic  3.04 us (7%)
  local copies, waits for them, and re-layouts  1.8 us (4%)
  matrix products  0.44 us (1%)
    all_to_all x1, blocking collectives, gram_route(): lax.all_to_all(pieces, ('grp', 'mod'), split_axis=0, concat_axis=0, tiled...  15.3 us
    ppermute x6, starting transfers between devices, xor_send(): return lax.ppermute(value, axis, pairs)  8.9 us
    ppermute x6, waiting for transfers between devices, xor_send(): return lax.ppermute(value, axis, pairs)  7.59 us
    pallas_call x1, Pallas kernels, gram_route(): pl.pallas_call(functools.partial(combine_kernel, rows), out_shape=jax.Sha...  5.13 us
    select_n x1, other arithmetic, local_features(): jnp.where(live_mask[:, :, None, None], token_block[:, :, :, half_width:],...  1.3 us
    select_n x2, other arithmetic, gram_route(): ordered = jnp.take(features, module_order, axis=0)  0.91 us
  transfers between devices with their start and end apart: 6, of which 4 were waited for; matrix products, arithmetic and copies ran while one was open for 0% of the time, Pallas kernels for 0%

profile of v1, /device:TPU:0, one launch (start us, length us, event | category | flops | bytes accessed | tf_op | source)
XLA Modules:
  0.0 42.3 jit_solution(4004740000782297530)
XLA Ops:
  0.0 0.7 %compare_select_fusion = s32[8]{0:T(128)S(1)} fusion(s32[8]{0:T(128)} %param.7), kind=kLoop, calls=%fused_computation.12 | loop fusion | flops 24 | bytes 64 | tf_op jit(solution)/shard_map/jit(_take)/jit(_where)/select_n | solution.py:170
  0.7 0.6 %copy-done.3 = s32[2]{0:T(128)S(1)} copy-done((s32[2]{0:T(128)S(1)}, s32[2]{0:T(128)}, u32[]{:S(2)}) %copy-start.3) | copy-done | bytes 32
  1.4 0.1 iota_compare_fusion
  1.5 1.3 %slice_select_fusion = (bf16[2,64,8,64]{3,2,1,0:T(8,128)(2,1)S(1)}, bf16[2,64,8,64]{3,2,1,0:T(8,128)(2,1)S(1)}) fusion(bf16[2,64,8,128]{3,2,1,0:T(8,128)(2,1)} %param.5, pred[2,64]{1,0:T(4,128)(4,1)S(1)} %iota_compare_fusion), kind=kLoop, calls=%fused_computation.4 | loop fusion | flops 65536 | bytes 524416 | tf_op jit(solution)/shard_map/jit(_where)/select_n | solution.py:201
  2.8 0.3 convolution_convert_fusion
  3.0 0.2 convert_element_type.17
  3.3 0.8 %gather_fusion = bf16[8,2,4096]{2,1,0:T(2,128)(2,1)S(1)} fusion(bf16[8,2,4096]{2,1,0:T(2,128)(2,1)S(1)} %convert_element_type.17, s32[1024]{0:T(1024)S(1)} %pad_clamp_fusion), kind=kCustom, calls=%fused_computation | custom fusion | bytes 262176 | tf_op jit(solution)/shard_map/jit(_take)/gather | solution.py:170
  4.1 0.2 broadcast_select_fusion
  4.3 15.3 %all_to_all.5 = bf16[32,2,1024]{2,1,0:T(2,128)(2,1)S(1)} all-to-all(bf16[32,2,1024]{2,1,0:T(2,128)(2,1)S(1)} %bitcast.22), channel_id=1, replica_groups=mesh['grp'=4,'mod'=8] {'grp','mod'}, dimensions={0} | all-to-all | bytes 262144 | tf_op jit(solution)/shard_map/all_to_all | solution.py:173
  19.6 0.1 reshape.87.leaf_ref
  19.7 0.2 fusion.2.near_ref
  19.9 0.7 %collective-permute-start = (f32[64,64]{1,0:T(8,128)S(1)}, f32[64,64]{1,0:T(8,128)S(1)}, u32[]{:S(2)}, u32[]{:S(2)}) collective-permute-start(f32[64,64]{1,0:T(8,128)S(1)} %fusion.2.near_ref), channel_id=1, source_target_pairs={{0,8},{8,0},{16,24},{24,16},{1,9},{9,1},{17,25},{25,17},{2,10},{10... | collective-permute-start | bytes 49160 | tf_op jit(solution)/shard_map/ppermute | solution.py:22
  20.6 1.2 %collective-permute-start.1 = (f32[64,64]{1,0:T(8,128)S(1)}, f32[64,64]{1,0:T(8,128)S(1)}, u32[]{:S(2)}, u32[]{:S(2)}) collective-permute-start(f32[64,64]{1,0:T(8,128)S(1)} %fusion.2.near_ref), channel_id=1, source_target_pairs={{0,16},{8,24},{16,0},{24,8},{1,17},{9,25},{17,1},{25,9},{2,18},{10... | collective-permute-start | bytes 49160 | tf_op jit(solution)/shard_map/ppermute | solution.py:22
  21.8 2.5 %collective-permute-start.2 = (f32[64,64]{1,0:T(8,128)S(1)}, f32[64,64]{1,0:T(8,128)S(1)}, u32[]{:S(2)}, u32[]{:S(2)}) collective-permute-start(f32[64,64]{1,0:T(8,128)S(1)} %fusion.2.near_ref), channel_id=1, source_target_pairs={{0,24},{8,16},{16,8},{24,0},{1,25},{9,17},{17,9},{25,1},{2,26},{10... | collective-permute-start | bytes 49160 | tf_op jit(solution)/shard_map/ppermute | solution.py:22
  24.3 0.0 collective-permute-done.a_ref
  24.3 1.9 %collective-permute-done.1.b_ref = f32[64,64]{1,0:T(8,128)S(1)} collective-permute-done((f32[64,64]{1,0:T(8,128)S(1)}, f32[64,64]{1,0:T(8,128)S(1)}, u32[]{:S(2)}, u32[]{:S(2)}) %collective-permute-start.1) | collective-permute-done | bytes 16416 | tf_op jit(solution)/shard_map/ppermute | solution.py:22
  26.2 1.3 %collective-permute-done.2.c_ref = f32[64,64]{1,0:T(8,128)S(1)} collective-permute-done((f32[64,64]{1,0:T(8,128)S(1)}, f32[64,64]{1,0:T(8,128)S(1)}, u32[]{:S(2)}, u32[]{:S(2)}) %collective-permute-start.2) | collective-permute-done | bytes 16416 | tf_op jit(solution)/shard_map/ppermute | solution.py:22
  27.6 5.1 %shard_map.55 = bf16[64,1024]{1,0:T(8,128)(2,1)S(1)} custom-call(f32[64,64]{1,0:T(8,128)S(1)} %fusion.2.near_ref, f32[64,64]{1,0:T(8,128)S(1)} %collective-permute-done.a_ref, f32[64,64]{1,0:T(8,128)S(1)} %collective-permute-done.1.b_ref, f32[64,64]{1,0:T(8,128)S(1)} %collective-permute-done.2.c_ref, f32[16,32]{1,0:T(8,128)S(1)} %copy-done.1, ...), custom_call_target="tpu_custom_call" | custom-call | tf_op jit(solution)/shard_map/pallas_call | solution.py:181
  32.7 0.1 collective-permute-start.3
  32.8 3.0 %collective-permute-start.4 = (bf16[16,1024]{1,0:T(8,128)(2,1)S(1)}, bf16[16,1024]{1,0:T(8,128)(2,1)S(1)}, u32[]{:S(2)}, u32[]{:S(2)}) collective-permute-start(bf16[16,1024]{1,0:T(8,128)(2,1)S(1)} %get-tuple-element.13), channel_id=1, source_target_pairs={{0,16},{8,24},{16,0},{24,8},{1,17},{9,25},{17,1},{25,9},{2,18},{10... | collective-permute-start | bytes 98312 | tf_op jit(solution)/shard_map/ppermute | solution.py:22
  35.8 1.3 %collective-permute-start.5 = (bf16[16,1024]{1,0:T(8,128)(2,1)S(1)}, bf16[16,1024]{1,0:T(8,128)(2,1)S(1)}, u32[]{:S(2)}, u32[]{:S(2)}) collective-permute-start(bf16[16,1024]{1,0:T(8,128)(2,1)S(1)} %get-tuple-element.12), channel_id=1, source_target_pairs={{0,24},{8,16},{16,8},{24,0},{1,25},{9,17},{17,9},{25,1},{2,26},{10... | collective-permute-start | bytes 98312 | tf_op jit(solution)/shard_map/ppermute | solution.py:22
  37.2 0.6 %collective-permute-done.4 = bf16[16,1024]{1,0:T(8,128)(2,1)S(1)} collective-permute-done((bf16[16,1024]{1,0:T(8,128)(2,1)S(1)}, bf16[16,1024]{1,0:T(8,128)(2,1)S(1)}, u32[]{:S(2)}, u32[]{:S(2)}) %collective-permute-start.4) | collective-permute-done | bytes 32800 | tf_op jit(solution)/shard_map/ppermute | solution.py:22
  37.7 3.8 %collective-permute-done.5 = bf16[16,1024]{1,0:T(8,128)(2,1)S(1)} collective-permute-done((bf16[16,1024]{1,0:T(8,128)(2,1)S(1)}, bf16[16,1024]{1,0:T(8,128)(2,1)S(1)}, u32[]{:S(2)}, u32[]{:S(2)}) %collective-permute-start.5) | collective-permute-done | bytes 32800 | tf_op jit(solution)/shard_map/ppermute | solution.py:22
  41.6 0.7 %maximum_convert_fusion = f32[1,16,4096]{2,1,0:T(8,128)} fusion(bf16[1,16,1024]{2,1,0:T(8,128)(2,1)S(1)} %get-tuple-element.8, bf16[1,16,1024]{2,1,0:T(8,128)(2,1)S(1)} %get-tuple-element.9, bf16[1,16,1024]{2,1,0:T(8,128)(2,1)S(1)} %get-tuple-element.10, bf16[1,16,1024]{2,1,0:T(8,128)(2,1)S(1)} %get-tuple-element.7), kind=kLoop, calls=%fused_computation.7 | loop fusion | flops 524288 | bytes 393216 | tf_op jit(solution)/shard_map/convert_element_type | solution.py:194
  (13 shorter events, 0.1 us)
Async XLA Ops:
  0.0 0.7 %copy-start.2 = (s32[8]{0:T(128)S(1)}, s32[8]{0:T(128)}, u32[]{:S(2)}) copy-start(s32[8]{0:T(128)} %param.7) | copy-start | bytes 100
  0.7 0.7 %copy-start.3 = (s32[2]{0:T(128)S(1)}, s32[2]{0:T(128)}, u32[]{:S(2)}) copy-start(s32[2]{0:T(128)} %param.6) | copy-start | bytes 28
  19.9 4.5 %collective-permute-start = (f32[64,64]{1,0:T(8,128)S(1)}, f32[64,64]{1,0:T(8,128)S(1)}, u32[]{:S(2)}, u32[]{:S(2)}) collective-permute-start(f32[64,64]{1,0:T(8,128)S(1)} %fusion.2.near_ref), channel_id=1, source_target_pairs={{0,8},{8,0},{16,24},{24,16},{1,9},{9,1},{17,25},{25,17},{2,10},{10... | collective-permute-start | bytes 49160 | tf_op jit(solution)/shard_map/ppermute | solution.py:22
  20.6 5.6 %collective-permute-start.1 = (f32[64,64]{1,0:T(8,128)S(1)}, f32[64,64]{1,0:T(8,128)S(1)}, u32[]{:S(2)}, u32[]{:S(2)}) collective-permute-start(f32[64,64]{1,0:T(8,128)S(1)} %fusion.2.near_ref), channel_id=1, source_target_pairs={{0,16},{8,24},{16,0},{24,8},{1,17},{9,25},{17,1},{25,9},{2,18},{10... | collective-permute-start | bytes 49160 | tf_op jit(solution)/shard_map/ppermute | solution.py:22
  21.8 5.7 %collective-permute-start.2 = (f32[64,64]{1,0:T(8,128)S(1)}, f32[64,64]{1,0:T(8,128)S(1)}, u32[]{:S(2)}, u32[]{:S(2)}) collective-permute-start(f32[64,64]{1,0:T(8,128)S(1)} %fusion.2.near_ref), channel_id=1, source_target_pairs={{0,24},{8,16},{16,8},{24,0},{1,25},{9,17},{17,9},{25,1},{2,26},{10... | collective-permute-start | bytes 49160 | tf_op jit(solution)/shard_map/ppermute | solution.py:22
  24.3 3.2 %copy-start = (f32[32,64]{1,0:T(8,128)S(1)}, f32[32,64]{1,0:T(8,128)}, u32[]{:S(2)}) copy-start(f32[32,64]{1,0:T(8,128)} %constant.53.clone.pair_ref) | copy-start | bytes 24580
  24.3 3.2 %copy-start.1 = (f32[16,32]{1,0:T(8,128)S(1)}, f32[16,32]{1,0:T(8,128)}, u32[]{:S(2)}) copy-start(f32[16,32]{1,0:T(8,128)} %constant.52.clone.start_ref) | copy-start | bytes 6148
  32.7 4.5 %collective-permute-start.3 = (bf16[16,1024]{1,0:T(8,128)(2,1)S(1)}, bf16[16,1024]{1,0:T(8,128)(2,1)S(1)}, u32[]{:S(2)}, u32[]{:S(2)}) collective-permute-start(bf16[16,1024]{1,0:T(8,128)(2,1)S(1)} %get-tuple-element.14), channel_id=1, source_target_pairs={{0,8},{8,0},{16,24},{24,16},{1,9},{9,1},{17,25},{25,17},{2,10},{10... | collective-permute-start | bytes 98312 | tf_op jit(solution)/shard_map/ppermute | solution.py:22
  32.8 4.9 %collective-permute-start.4 = (bf16[16,1024]{1,0:T(8,128)(2,1)S(1)}, bf16[16,1024]{1,0:T(8,128)(2,1)S(1)}, u32[]{:S(2)}, u32[]{:S(2)}) collective-permute-start(bf16[16,1024]{1,0:T(8,128)(2,1)S(1)} %get-tuple-element.13), channel_id=1, source_target_pairs={{0,16},{8,24},{16,0},{24,8},{1,17},{9,25},{17,1},{25,9},{2,18},{10... | collective-permute-start | bytes 98312 | tf_op jit(solution)/shard_map/ppermute | solution.py:22
  35.8 5.7 %collective-permute-start.5 = (bf16[16,1024]{1,0:T(8,128)(2,1)S(1)}, bf16[16,1024]{1,0:T(8,128)(2,1)S(1)}, u32[]{:S(2)}, u32[]{:S(2)}) collective-permute-start(bf16[16,1024]{1,0:T(8,128)(2,1)S(1)} %get-tuple-element.12), channel_id=1, source_target_pairs={{0,24},{8,16},{16,8},{24,0},{1,25},{9,17},{17,9},{25,1},{2,26},{10... | collective-permute-start | bytes 98312 | tf_op jit(solution)/shard_map/ppermute | solution.py:22

commit v2 on v1

--- a/solution.py
+++ b/solution.py
@@ -131,8 +131,8 @@
     return moved
 
 
-def combine_kernel(rows, near_ref, a_ref, b_ref, c_ref, start_ref, pair_ref, leaf_ref, out_ref):
-    gram = (near_ref[...] + a_ref[...]) + (b_ref[...] + c_ref[...])
+def combine_kernel(rows, gram_ref, start_ref, pair_ref, leaf_ref, out_ref):
+    gram = gram_ref[...]
     count = gram.shape[0]
     half = count // 2
     r = lax.broadcasted_iota(jnp.int32, gram.shape, 0)
@@ -173,7 +173,7 @@
     leaf = lax.all_to_all(pieces, ("grp", "mod"), split_axis=0, concat_axis=0, tiled=True)
     leaf = leaf.reshape(count, width // groups)
     gram = lax.dot_general(leaf, leaf, (((1,), (1,)), ((), ())), preferred_element_type=jnp.float32)
-    others = [xor_send(gram, "grp", mask) for mask in range(1, groups)]
+    gram = lax.psum(gram, "grp")
     start = start_basis(2 * rows, rows).T
     pair = np.zeros((2 * rows, 4 * rows), np.float32)
     pair[:rows, : 2 * rows] = start
@@ -182,16 +182,10 @@
         functools.partial(combine_kernel, rows),
         out_shape=jax.ShapeDtypeStruct(leaf.shape, jnp.bfloat16),
         compiler_params=pltpu.CompilerParams(vmem_limit_bytes=32 * 1024 * 1024),
-    )(gram, *others, jnp.asarray(start), jnp.asarray(pair), leaf)
+    )(gram, jnp.asarray(start), jnp.asarray(pair), leaf)
     blocks = out.reshape(groups, rows, width // groups)
-    me = lax.axis_index("grp")
-    received = [lax.dynamic_index_in_dim(blocks, me, 0, keepdims=False)]
-    for mask in range(1, groups):
-        mine = lax.dynamic_index_in_dim(blocks, me ^ mask, 0, keepdims=False)
-        received.append(xor_send(mine, "grp", mask))
-    received = jnp.stack(received)
-    chunks = [lax.dynamic_index_in_dim(received, me ^ g, 0, keepdims=False) for g in range(groups)]
-    return jnp.concatenate(chunks, axis=1).astype(jnp.float32)[None]
+    received = lax.all_to_all(blocks, "grp", split_axis=0, concat_axis=0, tiled=True)
+    return received.transpose(1, 0, 2).reshape(1, rows, width).astype(jnp.float32)
 
 
 def local_features(token_block, live_counts):

time: 42.5 us -> 51.8 us (1.22)
  blocking collectives: 15.3 us -> 40.7 us
  starting transfers between devices: 8.9 us -> 0 us
  waiting for transfers between devices: 7.59 us -> 0 us
  local copies, waits for them, and re-layouts: 1.8 us -> 2.82 us
  other arithmetic: 3.04 us -> 2.32 us
    psum x0 -> x1, blocking collectives: none -> 17 us  [gram_route(): gram = lax.psum(gram, 'grp')]
    ppermute x6 -> x0, starting transfers between devices: 8.9 us -> none  [xor_send(): return lax.ppermute(value, axis, pairs)]
    all_to_all x0 -> x1, blocking collectives: none -> 8.31 us  [gram_route(): lax.all_to_all(blocks, 'grp', split_axis=0, concat_axis=0, tiled=True)]
    ppermute x6 -> x0, waiting for transfers between devices: 7.59 us -> none  [xor_send(): return lax.ppermute(value, axis, pairs)]
    convert_element_type x0 -> x2, local copies, waits for them, and re-layouts: none -> 1.06 us  [gram_route(): received.transpose(1, 0, 2).reshape(1, rows, width).astype(jnp.float32)]
    convert_element_type x1, other arithmetic: 0.72 us -> 0.02 us  [gram_route(): received.transpose(1, 0, 2).reshape(1, rows, width).astype(jnp.float32)]
  transfers between devices with their start and end apart: 6 -> 0, of which waited for: 4 -> 0; matrix products, arithmetic and copies ran while one was open for 0% -> 0% of each run, Pallas kernels for 0% -> 0%
where the time goes in v2:
time: 51.8 us; the launch traced here: 51.5 us
  blocking collectives  40.7 us (79%)
  Pallas kernels  5.13 us (10%)
  local copies, waits for them, and re-layouts  2.82 us (5%)
  other arithmetic  2.32 us (4%)
    psum x1, blocking collectives, gram_route(): gram = lax.psum(gram, 'grp')  17 us
    all_to_all x1, blocking collectives, gram_route(): lax.all_to_all(pieces, ('grp', 'mod'), split_axis=0, concat_axis=0, tiled...  15.3 us
    all_to_all x1, blocking collectives, gram_route(): lax.all_to_all(blocks, 'grp', split_axis=0, concat_axis=0, tiled=True)  8.31 us
    pallas_call x1, Pallas kernels, gram_route(): pl.pallas_call(functools.partial(combine_kernel, rows), out_shape=jax.Sha...  5.13 us
    select_n x1, other arithmetic, local_features(): jnp.where(live_mask[:, :, None, None], token_block[:, :, :, half_width:],...  1.3 us
    convert_element_type x2, local copies, waits for them, and re-layouts, gram_route(): received.transpose(1, 0, 2).reshape(1, rows, width).astype(jnp.float32)  1.06 us

profile of v2, /device:TPU:0, one launch (start us, length us, event | category | flops | bytes accessed | tf_op | source)
XLA Modules:
  0.0 51.5 jit_solution(1538821350444128207)
XLA Ops:
  0.0 0.0 copy-start.2
  0.0 0.7 %compare_select_fusion = s32[8]{0:T(128)S(1)} fusion(s32[8]{0:T(128)} %param.7), kind=kLoop, calls=%fused_computation.8 | loop fusion | flops 24 | bytes 64 | tf_op jit(solution)/shard_map/jit(_take)/jit(_where)/select_n | solution.py:170
  0.7 0.0 copy-done.2
  0.7 0.0 copy-start.3
  0.7 0.6 %copy-done.3 = s32[2]{0:T(128)S(1)} copy-done((s32[2]{0:T(128)S(1)}, s32[2]{0:T(128)}, u32[]{:S(2)}) %copy-start.3) | copy-done | bytes 32
  1.4 0.1 iota_compare_fusion
  1.5 1.3 %slice_select_fusion = (bf16[2,64,8,64]{3,2,1,0:T(8,128)(2,1)S(1)}, bf16[2,64,8,64]{3,2,1,0:T(8,128)(2,1)S(1)}) fusion(bf16[2,64,8,128]{3,2,1,0:T(8,128)(2,1)} %param.5, pred[2,64]{1,0:T(4,128)(4,1)S(1)} %iota_compare_fusion), kind=kLoop, calls=%fused_computation.5 | loop fusion | flops 65536 | bytes 524416 | tf_op jit(solution)/shard_map/jit(_where)/select_n | solution.py:195
  2.8 0.3 convolution_convert_fusion
  3.0 0.2 convert_element_type.24
  3.3 0.8 %gather_fusion = bf16[8,2,4096]{2,1,0:T(2,128)(2,1)S(1)} fusion(bf16[8,2,4096]{2,1,0:T(2,128)(2,1)S(1)} %convert_element_type.24, s32[1024]{0:T(1024)S(1)} %pad_clamp_fusion), kind=kCustom, calls=%fused_computation | custom fusion | bytes 262176 | tf_op jit(solution)/shard_map/jit(_take)/gather | solution.py:170
  4.1 0.2 broadcast_select_fusion
  4.3 15.3 %all_to_all.10 = bf16[32,2,1024]{2,1,0:T(2,128)(2,1)S(1)} all-to-all(bf16[32,2,1024]{2,1,0:T(2,128)(2,1)S(1)} %bitcast.15), channel_id=1, replica_groups=mesh['grp'=4,'mod'=8] {'grp','mod'}, dimensions={0} | all-to-all | bytes 262144 | tf_op jit(solution)/shard_map/all_to_all | solution.py:173
  19.6 0.1 reshape.55.leaf_ref
  19.7 0.2 fusion.2
  19.9 0.0 copy-start
  19.9 0.0 copy-start.1
  19.9 17.0 %psum.7.gram_ref = f32[64,64]{1,0:T(8,128)S(1)} all-reduce(f32[64,64]{1,0:T(8,128)S(1)} %fusion.2), channel_id=1, replica_groups=mesh['grp'=4,'mod'=8] {'grp'}, use_global_device_ids=true, to_apply=%region_0.1 | all-reduce | flops 4096 | bytes 32768 | tf_op jit(solution)/shard_map/psum | solution.py:176
  37.0 0.0 copy-done
  37.0 0.0 copy-done.1
  37.0 5.1 %shard_map.55 = bf16[64,1024]{1,0:T(8,128)(2,1)S(1)} custom-call(f32[64,64]{1,0:T(8,128)S(1)} %psum.7.gram_ref, f32[16,32]{1,0:T(8,128)S(1)} %copy-done.1, f32[32,64]{1,0:T(8,128)S(1)} %copy-done, bf16[64,1024]{1,0:T(8,128)(2,1)S(1)} %reshape.55.leaf_ref), custom_call_target="tpu_custom_call" | custom-call | tf_op jit(solution)/shard_map/pallas_call | solution.py:181
  42.1 8.3 %all_to_all.11 = bf16[4,16,1024]{2,1,0:T(8,128)(2,1)S(1)} all-to-all(bf16[4,16,1024]{2,1,0:T(8,128)(2,1)S(1)} %bitcast.13), channel_id=1, replica_groups=mesh['grp'=4,'mod'=8] {'grp'}, dimensions={0} | all-to-all | bytes 262144 | tf_op jit(solution)/shard_map/all_to_all | solution.py:187
  50.4 0.2 copy.9
  50.6 0.9 %reshape.57 = f32[1,16,4096]{2,1,0:T(8,128)} reshape(f32[16,4,1024]{2,1,0:T(4,128)S(1)} %copy.9) | data formatting | bytes 524288 | tf_op jit(solution)/shard_map/convert_element_type | solution.py:188
  (3 shorter events, 0.0 us)
Async XLA Ops:
  0.0 0.7 %copy-start.2 = (s32[8]{0:T(128)S(1)}, s32[8]{0:T(128)}, u32[]{:S(2)}) copy-start(s32[8]{0:T(128)} %param.7) | copy-start | bytes 100
  0.7 0.7 %copy-start.3 = (s32[2]{0:T(128)S(1)}, s32[2]{0:T(128)}, u32[]{:S(2)}) copy-start(s32[2]{0:T(128)} %param.6) | copy-start | bytes 28
  19.9 17.1 %copy-start = (f32[32,64]{1,0:T(8,128)S(1)}, f32[32,64]{1,0:T(8,128)}, u32[]{:S(2)}) copy-start(f32[32,64]{1,0:T(8,128)} %constant.23.clone.pair_ref) | copy-start | bytes 24580
  19.9 17.1 %copy-start.1 = (f32[16,32]{1,0:T(8,128)S(1)}, f32[16,32]{1,0:T(8,128)}, u32[]{:S(2)}) copy-start(f32[16,32]{1,0:T(8,128)} %constant.22.clone.start_ref) | copy-start | bytes 6148

commit v3 on v2

--- a/solution.py
+++ b/solution.py
@@ -131,9 +131,10 @@
     return moved
 
 
-def combine_kernel(rows, gram_ref, start_ref, pair_ref, leaf_ref, out_ref):
-    gram = gram_ref[...]
-    count = gram.shape[0]
+def combine_kernel(rows, start_ref, pair_ref, leaf_ref, out_ref, change_ref):
+    count, width = leaf_ref.shape
+    leaf = leaf_ref[...]
+    gram = lax.dot_general(leaf, leaf, (((1,), (1,)), ((), ())), preferred_element_type=jnp.float32)
     half = count // 2
     r = lax.broadcasted_iota(jnp.int32, gram.shape, 0)
     c = lax.broadcasted_iota(jnp.int32, gram.shape, 1)
@@ -152,14 +153,15 @@
     for j in range(rows):
         columns[j][j // 8] = columns[j][j // 8] + jnp.where(row == j % 8, damping, 0.0)
     solved = eliminate(columns, jnp.concatenate([projected, weights], axis=1))
-    change = lax.dot_general(
+    change_ref[...] = lax.dot_general(
         solved[:, :count], solved[:, count:], (((0,), (0,)), ((), ())), precision=HI, preferred_element_type=jnp.float32
     )
+    own = pl.ds(pl.multiple_of(lax.axis_index("grp") * rows, rows), rows)
+    change = change_ref[own, :]
     top = change.astype(jnp.bfloat16)
     rest = (change - top.astype(jnp.float32)).astype(jnp.bfloat16)
-    leaf = leaf_ref[...]
     moved = jnp.dot(top, leaf, preferred_element_type=jnp.float32) + jnp.dot(rest, leaf, preferred_element_type=jnp.float32)
-    out_ref[...] = (leaf.astype(jnp.float32) - moved).astype(out_ref.dtype)
+    out_ref[0] = leaf_ref[own, :].astype(jnp.float32) - moved
 
 
 def gram_route(features, module_order):
@@ -168,24 +170,19 @@
     rows = owners * own
     count = groups * rows
     ordered = jnp.take(features, module_order, axis=0)
-    pieces = ordered.reshape(modules, own, groups, width // groups).transpose(2, 0, 1, 3)
-    pieces = pieces.reshape(groups * modules, own, width // groups)
+    pieces = jnp.broadcast_to(ordered[None], (groups, modules, own, width)).reshape(groups * modules, own, width)
     leaf = lax.all_to_all(pieces, ("grp", "mod"), split_axis=0, concat_axis=0, tiled=True)
-    leaf = leaf.reshape(count, width // groups)
-    gram = lax.dot_general(leaf, leaf, (((1,), (1,)), ((), ())), preferred_element_type=jnp.float32)
-    gram = lax.psum(gram, "grp")
+    leaf = leaf.reshape(count, width)
     start = start_basis(2 * rows, rows).T
     pair = np.zeros((2 * rows, 4 * rows), np.float32)
     pair[:rows, : 2 * rows] = start
     pair[rows:, 2 * rows :] = start
-    out = pl.pallas_call(
+    return pl.pallas_call(
         functools.partial(combine_kernel, rows),
-        out_shape=jax.ShapeDtypeStruct(leaf.shape, jnp.bfloat16),
+        out_shape=jax.ShapeDtypeStruct((1, rows, width), jnp.float32),
+        scratch_shapes=[pltpu.VMEM((count, count), jnp.float32)],
         compiler_params=pltpu.CompilerParams(vmem_limit_bytes=32 * 1024 * 1024),
-    )(gram, jnp.asarray(start), jnp.asarray(pair), leaf)
-    blocks = out.reshape(groups, rows, width // groups)
-    received = lax.all_to_all(blocks, "grp", split_axis=0, concat_axis=0, tiled=True)
-    return received.transpose(1, 0, 2).reshape(1, rows, width).astype(jnp.float32)
+    )(jnp.asarray(start), jnp.asarray(pair), leaf)
 
 
 def local_features(token_block, live_counts):

time: 51.8 us -> 34.7 us (0.67)
  blocking collectives: 40.7 us -> 22.7 us
  Pallas kernels: 5.13 us -> 6.27 us
    psum x1 -> x0, blocking collectives: 17 us -> none  [gram_route(): gram = lax.psum(gram, 'grp')]
    all_to_all x1 -> x0, blocking collectives: 8.31 us -> none  [gram_route(): lax.all_to_all(blocks, 'grp', split_axis=0, concat_axis=0, tiled=True)]
    all_to_all x1, blocking collectives: 15.3 us -> 22.7 us  [gram_route(): lax.all_to_all(pieces, ('grp', 'mod'), split_axis=0, concat_axis=0, tiled...]
    pallas_call x1, Pallas kernels: 5.13 us -> 6.27 us  [gram_route(): pl.pallas_call(functools.partial(combine_kernel, rows), out_shape=jax.Sha...]
    convert_element_type x2 -> x0, local copies, waits for them, and re-layouts: 1.06 us -> none  [gram_route(): received.transpose(1, 0, 2).reshape(1, rows, width).astype(jnp.float32)]
    and x1, other arithmetic: 0.01 us -> 0.73 us  [gram_route(): ordered = jnp.take(features, module_order, axis=0)]
    select_n x2, other arithmetic: 0.91 us -> 0.19 us  [gram_route(): ordered = jnp.take(features, module_order, axis=0)]
where the time goes in v3:
time: 34.7 us; the launch traced here: 34.4 us
  blocking collectives  22.7 us (65%)
  Pallas kernels  6.27 us (18%)
  local copies, waits for them, and re-layouts  2.87 us (8%)
  other arithmetic  2.3 us (7%)
    all_to_all x1, blocking collectives, gram_route(): lax.all_to_all(pieces, ('grp', 'mod'), split_axis=0, concat_axis=0, tiled...  22.7 us
    pallas_call x1, Pallas kernels, gram_route(): pl.pallas_call(functools.partial(combine_kernel, rows), out_shape=jax.Sha...  6.27 us
    select_n x1, other arithmetic, local_features(): jnp.where(live_mask[:, :, None, None], token_block[:, :, :, half_width:],...  1.3 us
    unnamed x8, local copies, waits for them, and re-layouts  1.16 us
    gather x1, local copies, waits for them, and re-layouts, gram_route(): ordered = jnp.take(features, module_order, axis=0)  0.81 us
    and x1, other arithmetic, gram_route(): ordered = jnp.take(features, module_order, axis=0)  0.73 us

profile of v3, /device:TPU:0, one launch (start us, length us, event | category | flops | bytes accessed | tf_op | source)
XLA Modules:
  0.0 34.4 jit_solution(16971443259730134512)
XLA Ops:
  0.0 0.0 copy-start.2
  0.0 0.7 %compare_and_fusion = pred[8]{0:T(512)(128)(4,1)S(1)} fusion(s32[8]{0:T(128)} %param.7), kind=kLoop, calls=%fused_computation.8 | loop fusion | flops 48 | bytes 40 | tf_op jit(solution)/shard_map/jit(_take)/and | solution.py:172
  0.7 0.0 copy-done.2
  0.7 0.0 copy-start.3
  0.8 0.6 %copy-done.3 = s32[2]{0:T(128)S(1)} copy-done((s32[2]{0:T(128)S(1)}, s32[2]{0:T(128)}, u32[]{:S(2)}) %copy-start.3) | copy-done | bytes 32
  1.4 0.1 iota_compare_fusion
  1.5 1.3 %slice_select_fusion = (bf16[2,64,8,64]{3,2,1,0:T(8,128)(2,1)S(1)}, bf16[2,64,8,64]{3,2,1,0:T(8,128)(2,1)S(1)}) fusion(bf16[2,64,8,128]{3,2,1,0:T(8,128)(2,1)} %param.5, pred[2,64]{1,0:T(4,128)(4,1)S(1)} %iota_compare_fusion), kind=kLoop, calls=%fused_computation.4 | loop fusion | flops 65536 | bytes 524416 | tf_op jit(solution)/shard_map/jit(_where)/select_n | solution.py:192
  2.8 0.3 convolution_convert_fusion
  3.1 0.2 convert_element_type.7
  3.3 0.8 %gather_fusion = bf16[8,2,4096]{2,1,0:T(2,128)(2,1)S(1)} fusion(bf16[8,2,4096]{2,1,0:T(2,128)(2,1)S(1)} %convert_element_type.7, s32[1024]{0:T(1024)S(1)} %pad_clamp_fusion), kind=kCustom, calls=%fused_computation | custom fusion | bytes 262176 | tf_op jit(solution)/shard_map/jit(_take)/gather | solution.py:172
  4.1 0.2 broadcast_select_fusion
  4.3 0.5 %broadcast_in_dim.38 = bf16[4,8,2,4096]{3,2,1,0:T(2,128)(2,1)S(1)} broadcast(bf16[8,2,4096]{2,1,0:T(2,128)(2,1)S(1)} %broadcast_select_fusion), dimensions={1,2,3} | broadcast | bytes 655360 | tf_op jit(solution)/shard_map/broadcast_in_dim | solution.py:173
  4.8 22.7 %all_to_all.5 = bf16[32,2,4096]{2,1,0:T(2,128)(2,1)S(1)} all-to-all(bf16[32,2,4096]{2,1,0:T(2,128)(2,1)S(1)} %bitcast.3), channel_id=1, replica_groups=mesh['grp'=4,'mod'=8] {'grp','mod'}, dimensions={0} | all-to-all | bytes 1048576 | tf_op jit(solution)/shard_map/all_to_all | solution.py:174
  27.4 0.0 copy-start
  27.4 0.0 copy-start.1
  27.4 0.2 reshape.38.leaf_ref
  27.6 0.5 %copy-done = f32[32,64]{1,0:T(8,128)S(1)} copy-done((f32[32,64]{1,0:T(8,128)S(1)}, f32[32,64]{1,0:T(8,128)}, u32[]{:S(2)}) %copy-start) | copy-done | bytes 8216
  28.1 0.0 copy-done.1
  28.1 6.3 %shard_map.55 = f32[1,16,4096]{2,1,0:T(8,128)} custom-call(f32[16,32]{1,0:T(8,128)S(1)} %copy-done.1, f32[32,64]{1,0:T(8,128)S(1)} %copy-done, bf16[64,4096]{1,0:T(8,128)(2,1)S(1)} %reshape.38.leaf_ref), custom_call_target="tpu_custom_call" | custom-call | tf_op jit(solution)/shard_map/pallas_call | solution.py:180
  (2 shorter events, 0.0 us)
Async XLA Ops:
  0.0 0.7 %copy-start.2 = (s32[8]{0:T(128)S(1)}, s32[8]{0:T(128)}, u32[]{:S(2)}) copy-start(s32[8]{0:T(128)} %param.7) | copy-start | bytes 100
  0.7 0.7 %copy-start.3 = (s32[2]{0:T(128)S(1)}, s32[2]{0:T(128)}, u32[]{:S(2)}) copy-start(s32[2]{0:T(128)} %param.6) | copy-start | bytes 28
  27.4 0.7 %copy-start = (f32[32,64]{1,0:T(8,128)S(1)}, f32[32,64]{1,0:T(8,128)}, u32[]{:S(2)}) copy-start(f32[32,64]{1,0:T(8,128)} %constant.23.clone.pair_ref) | copy-start | bytes 24580
  27.4 0.7 %copy-start.1 = (f32[16,32]{1,0:T(8,128)S(1)}, f32[16,32]{1,0:T(8,128)}, u32[]{:S(2)}) copy-start(f32[16,32]{1,0:T(8,128)} %constant.22.clone.start_ref) | copy-start | bytes 6148

commit v4 on v3

--- a/solution.py
+++ b/solution.py
@@ -164,15 +164,59 @@
     out_ref[0] = leaf_ref[own, :].astype(jnp.float32) - moved
 
 
-def gram_route(features, module_order):
+def features_kernel(splits, lengths_ref, order_ref, tokens_ref, out_ref, held_ref):
+    examples, depth, full = tokens_ref.shape
+    half = full // 2
+    modules = order_ref.shape[0]
+    chunks = half * half // full
+    position = lax.broadcasted_iota(jnp.int32, (modules, depth), 1)
+    module = lax.broadcasted_iota(jnp.int32, (modules, depth), 0)
+    mine = lax.rem(position, modules) == module
+    lane = lax.broadcasted_iota(jnp.int32, (depth, full), 1)
+    for e in range(examples):
+        block = tokens_ref[e].astype(jnp.float32)
+        grads = block.T[half:]
+        live = jnp.logical_and(mine, position < lengths_ref[e] * modules)
+        rows = []
+        for o in range(half):
+            rows.append(jnp.where(live, grads[o : o + 1], 0.0).astype(jnp.bfloat16))
+        even = jnp.concatenate(rows[0::2], axis=0)
+        odd = jnp.concatenate(rows[1::2], axis=0)
+        left = jnp.where(lane < half, block, 0.0).astype(jnp.bfloat16)
+        right = jnp.where(lane < half, 0.0, pltpu.roll(block, half, 1)).astype(jnp.bfloat16)
+        flat = jnp.dot(even, left, preferred_element_type=jnp.float32) + jnp.dot(odd, right, preferred_element_type=jnp.float32)
+        for c in range(chunks):
+            held_ref[pl.ds(c * modules * examples + e, modules, stride=examples), :] = flat[c * modules : (c + 1) * modules]
+    groups = out_ref.shape[0]
+    span = chunks // splits
+    for slot in range(modules):
+        first = order_ref[slot] * examples
+        for c in range(chunks):
+            pair = held_ref[pl.ds(c * modules * examples + first, examples), :].astype(jnp.bfloat16)
+            for g in range(c // span, groups, splits):
+                out_ref[g, slot, :, (c % span) * full : (c % span + 1) * full] = pair
+
+
+def gram_route(tokens, lengths, module_order, splits=1):
     groups, owners = lax.axis_size("grp"), lax.axis_size("mod")
-    modules, own, width = features.shape
+    own, slots, modules, full = tokens.shape
+    width = (full // 2) ** 2
     rows = owners * own
     count = groups * rows
-    ordered = jnp.take(features, module_order, axis=0)
-    pieces = jnp.broadcast_to(ordered[None], (groups, modules, own, width)).reshape(groups * modules, own, width)
+    pieces = pl.pallas_call(
+        functools.partial(features_kernel, splits),
+        out_shape=jax.ShapeDtypeStruct((groups, modules, own, width // splits), jnp.bfloat16),
+        in_specs=[
+            pl.BlockSpec(memory_space=pltpu.SMEM),
+            pl.BlockSpec(memory_space=pltpu.SMEM),
+            pl.BlockSpec(memory_space=pltpu.VMEM),
+        ],
+        scratch_shapes=[pltpu.VMEM((own * modules * width // full, full), jnp.float32)],
+        compiler_params=pltpu.CompilerParams(vmem_limit_bytes=32 * 1024 * 1024),
+    )(lengths, module_order, tokens.reshape(own, slots * modules, full))
+    pieces = pieces.reshape(groups * modules, own, width // splits)
     leaf = lax.all_to_all(pieces, ("grp", "mod"), split_axis=0, concat_axis=0, tiled=True)
-    leaf = leaf.reshape(count, width)
+    leaf = leaf.reshape(count, width // splits)
     start = start_basis(2 * rows, rows).T
     pair = np.zeros((2 * rows, 4 * rows), np.float32)
     pair[:rows, : 2 * rows] = start
@@ -200,12 +244,11 @@
 
 
 def per_device(tokens, lengths, module_order):
-    features = local_features(tokens, lengths)
     groups, owners = lax.axis_size("grp"), lax.axis_size("mod")
-    rows = owners * features.shape[1]
-    if groups == 4 and rows == 16 and owners == features.shape[0]:
-        return gram_route(features, module_order)
-    return sketch_tree(features, module_order)
+    own, slots, modules, full = tokens.shape
+    if groups == 4 and owners * own == 16 and owners == modules == 8 and full == 128:
+        return gram_route(tokens, lengths, module_order)
+    return sketch_tree(local_features(tokens, lengths), module_order)
 
 
 def solution(mesh):

time: 34.7 us -> 33 us (0.951)
  other arithmetic: 2.3 us -> 0 us
  Pallas kernels: 6.27 us -> 7.71 us
  local copies, waits for them, and re-layouts: 2.87 us -> 2.33 us
    select_n x3 -> x0, other arithmetic: 1.48 us -> none  [the longest x1 1.3 us: local_features(): jnp.where(live_mask[:, :, None, None], token_block[:, :, :, half_width:],...]
    pallas_call x0 -> x1, Pallas kernels: none -> 1.44 us  [gram_route(): pl.pallas_call(functools.partial(features_kernel, splits), out_shape=jax....]
    unnamed x8 -> x10, local copies, waits for them, and re-layouts: 1.16 us -> 2.14 us
    gather x1 -> x0, local copies, waits for them, and re-layouts: 0.81 us -> none  [gram_route(): ordered = jnp.take(features, module_order, axis=0)]
    and x1 -> x0, other arithmetic: 0.73 us -> none  [gram_route(): ordered = jnp.take(features, module_order, axis=0)]
    broadcast_in_dim x1 -> x0, local copies, waits for them, and re-layouts: 0.47 us -> none  [gram_route(): jnp.broadcast_to(ordered[None], (groups, modules, own, width))]
where the time goes in v4:
time: 33 us; the launch traced here: 32.7 us
  blocking collectives  22.7 us (69%)
  Pallas kernels  7.71 us (23%)
  local copies, waits for them, and re-layouts  2.33 us (7%)
    all_to_all x1, blocking collectives, gram_route(): lax.all_to_all(pieces, ('grp', 'mod'), split_axis=0, concat_axis=0, tiled...  22.7 us
    pallas_call x1, Pallas kernels, gram_route(): pl.pallas_call(functools.partial(combine_kernel, rows), out_shape=jax.Sha...  6.27 us
    unnamed x10, local copies, waits for them, and re-layouts  2.14 us
    pallas_call x1, Pallas kernels, gram_route(): pl.pallas_call(functools.partial(features_kernel, splits), out_shape=jax....  1.44 us

profile of v4, /device:TPU:0, one launch (start us, length us, event | category | flops | bytes accessed | tf_op | source)
XLA Modules:
  0.0 32.7 jit_solution(4098389502730257447)
XLA Ops:
  0.0 0.0 copy-start.4
  0.0 0.0 copy-start.3
  0.0 0.7 %copy-done.4 = s32[8]{0:T(128)S(1)} copy-done((s32[8]{0:T(128)S(1)}, s32[8]{0:T(128)}, u32[]{:S(2)}) %copy-start.4) | copy-done | bytes 56
  0.7 0.0 copy-done.3
  0.7 0.0 copy-start
  0.7 0.9 %copy-done = bf16[2,64,8,128]{3,2,1,0:T(8,128)(2,1)S(1)} copy-done((bf16[2,64,8,128]{3,2,1,0:T(8,128)(2,1)S(1)}, bf16[2,64,8,128]{3,2,1,0:T(8,128)(2,1)}, u32[]{:S(2)}) %copy-start) | copy-done | bytes 262168
  1.6 1.4 %shard_map.55 = bf16[4,8,2,4096]{3,2,1,0:T(2,128)(2,1)S(1)} custom-call(s32[2]{0:T(128)S(1)} %copy-done.3, s32[8]{0:T(128)S(1)} %copy-done.4, bf16[2,512,128]{2,1,0:T(8,128)(2,1)S(1)} %bitcast.3), custom_call_target="tpu_custom_call" | custom-call | tf_op jit(solution)/shard_map/pallas_call | solution.py:206
  3.1 22.7 %all_to_all.5 = bf16[32,2,4096]{2,1,0:T(2,128)(2,1)S(1)} all-to-all(bf16[32,2,4096]{2,1,0:T(2,128)(2,1)S(1)} %bitcast.2), channel_id=1, replica_groups=mesh['grp'=4,'mod'=8] {'grp','mod'}, dimensions={0} | all-to-all | bytes 1048576 | tf_op jit(solution)/shard_map/all_to_all | solution.py:218
  25.7 0.0 copy-start.1
  25.7 0.0 copy-start.2
  25.7 0.2 reshape.11.leaf_ref
  25.9 0.5 %copy-done.1 = f32[32,64]{1,0:T(8,128)S(1)} copy-done((f32[32,64]{1,0:T(8,128)S(1)}, f32[32,64]{1,0:T(8,128)}, u32[]{:S(2)}) %copy-start.1) | copy-done | bytes 8216
  26.4 0.0 copy-done.2
  26.4 6.3 %shard_map.56 = f32[1,16,4096]{2,1,0:T(8,128)} custom-call(f32[16,32]{1,0:T(8,128)S(1)} %copy-done.2, f32[32,64]{1,0:T(8,128)S(1)} %copy-done.1, bf16[64,4096]{1,0:T(8,128)(2,1)S(1)} %reshape.11.leaf_ref), custom_call_target="tpu_custom_call" | custom-call | tf_op jit(solution)/shard_map/pallas_call | solution.py:224
Async XLA Ops:
  0.0 0.7 %copy-start.4 = (s32[8]{0:T(128)S(1)}, s32[8]{0:T(128)}, u32[]{:S(2)}) copy-start(s32[8]{0:T(128)} %order_ref.1) | copy-start | bytes 100
  0.0 0.7 %copy-start.3 = (s32[2]{0:T(128)S(1)}, s32[2]{0:T(128)}, u32[]{:S(2)}) copy-start(s32[2]{0:T(128)} %lengths_ref.1) | copy-start | bytes 28
  0.7 0.9 %copy-start = (bf16[2,64,8,128]{3,2,1,0:T(8,128)(2,1)S(1)}, bf16[2,64,8,128]{3,2,1,0:T(8,128)(2,1)}, u32[]{:S(2)}) copy-start(bf16[2,64,8,128]{3,2,1,0:T(8,128)(2,1)} %param.5) | copy-start | bytes 786436
  25.7 0.7 %copy-start.1 = (f32[32,64]{1,0:T(8,128)S(1)}, f32[32,64]{1,0:T(8,128)}, u32[]{:S(2)}) copy-start(f32[32,64]{1,0:T(8,128)} %constant.5.clone.pair_ref) | copy-start | bytes 24580
  25.7 0.7 %copy-start.2 = (f32[16,32]{1,0:T(8,128)S(1)}, f32[16,32]{1,0:T(8,128)}, u32[]{:S(2)}) copy-start(f32[16,32]{1,0:T(8,128)} %constant.4.clone.start_ref) | copy-start | bytes 6148

commit v5 on v4

--- a/solution.py
+++ b/solution.py
@@ -1,4 +1,5 @@
 import functools
+import math
 
 import jax
 import jax.numpy as jnp
@@ -81,11 +82,30 @@
     return jnp.dot(a, b, precision=HI, preferred_element_type=jnp.float32)
 
 
-def spread_columns(gram, first, count, width):
+def start_rows(count, width, span):
+    j = lax.broadcasted_iota(jnp.int32, (count, width), 0)
+    i = lax.rem(lax.broadcasted_iota(jnp.int32, (count, width), 1), span)
+    turn = lax.rem((2 * i + 1) * (2 * j + 1), 8 * span)
+    folded = jnp.minimum(turn, 8 * span - turn)
+    angle = (2 * span - folded).astype(jnp.float32) * (math.pi / (4 * span))
+    square = angle * angle
+    series = jnp.full_like(angle, 1.0)
+    for n in range(12, 0, -2):
+        series = 1.0 - square * series * (1.0 / (n * (n + 1)))
+    return angle * series
+
+
+def spread(gram, problems, count, width):
+    lane = lax.broadcasted_iota(jnp.int32, (8, width), 1)
     columns = []
     for j in range(count):
-        column = gram[first : first + count, first + j : first + j + 1]
-        blocks = {b: jnp.broadcast_to(column[8 * b : 8 * b + 8], (8, width)) for b in range(j // 8, count // 8)}
+        blocks = {}
+        for b in range(j // 8, count // 8):
+            parts = [
+                jnp.broadcast_to(gram[8 * b : 8 * b + 8, k * count + j : k * count + j + 1], (8, width))
+                for k in range(problems)
+            ]
+            blocks[b] = parts[0] if problems == 1 else jnp.where(lane < width // 2, parts[0], parts[1])
         columns.append(blocks)
     return columns
 
@@ -96,65 +116,99 @@
     parts = [rhs[8 * b : 8 * b + 8] for b in range(count // 8)]
     row = lax.broadcasted_iota(jnp.int32, (8, width), 0)
     diag = [jnp.ones((8, width), jnp.float32) for _ in parts]
-    for p in range(count):
+    for p in range(0, count, 2):
         home, at = divmod(p, 8)
-        pivot_column = columns[p]
-        pivot = pivot_column[home][at : at + 1]
-        diag[home] = jnp.where(row == at, pivot, diag[home])
-        if p == count - 1:
-            break
-        inverse = 1.0 / pivot
-        factor = {}
-        for b in pivot_column:
-            scaled = pivot_column[b] * inverse
-            factor[b] = jnp.where(row > at, scaled, 0.0) if b == home else scaled
-        for j in range(p + 1, count):
-            along = pivot_column[j // 8][j % 8 : j % 8 + 1]
-            columns[j] = {b: block - factor[b] * along for b, block in columns[j].items()}
-        pivot_row = parts[home][at : at + 1]
-        for b in factor:
-            parts[b] = parts[b] - factor[b] * pivot_row
+        left, right = columns[p], columns[p + 1]
+        a = left[home][at : at + 1]
+        b = left[home][at + 1 : at + 2]
+        c = right[home][at + 1 : at + 2]
+        det = a * c - b * b
+        ratio = b / a
+        diag[home] = jnp.where(row == at, a, jnp.where(row == at + 1, c - b * ratio, diag[home]))
+        inverse = 1.0 / det
+        ia, ib, ic = c * inverse, b * inverse, a * inverse
+        low, high = {}, {}
+        for k in left:
+            low[k] = left[k] * ia - right[k] * ib
+            high[k] = right[k] * ic - left[k] * ib
+        for j in range(p + 2, count):
+            one = left[j // 8][j % 8 : j % 8 + 1]
+            two = right[j // 8][j % 8 : j % 8 + 1]
+            columns[j] = {k: block - (low[k] * one + high[k] * two) for k, block in columns[j].items()}
+        low[home] = jnp.where(row > at + 1, low[home], jnp.where(row == at + 1, ratio, 0.0))
+        high[home] = jnp.where(row > at + 1, high[home], 0.0)
+        first, second = parts[home][at : at + 1], parts[home][at + 1 : at + 2]
+        for k in low:
+            parts[k] = parts[k] - (low[k] * first + high[k] * second)
     return jnp.concatenate([part * lax.rsqrt(d) for part, d in zip(parts, diag)], axis=0)
 
 
-def orthogonal_iteration(start, kernel, problems):
-    rows = start.shape[0] // problems
-    moved = dot_nn(start, kernel)
-    for step in range(ITERS + 1):
-        gram = dot_nt(moved, moved)
-        onward = dot_nn(moved, kernel) if step < ITERS - 1 else moved
-        done = []
-        for k in range(problems):
-            columns = spread_columns(gram, k * rows, rows, onward.shape[1])
-            done.append(eliminate(columns, onward[k * rows : (k + 1) * rows]))
-        moved = jnp.concatenate(done, axis=0)
-    return moved
-
-
-def combine_kernel(rows, start_ref, pair_ref, leaf_ref, out_ref, change_ref):
-    count, width = leaf_ref.shape
-    leaf = leaf_ref[...]
-    gram = lax.dot_general(leaf, leaf, (((1,), (1,)), ((), ())), preferred_element_type=jnp.float32)
+def apart(value):
+    lane = lax.broadcasted_iota(jnp.int32, value.shape, 1)
+    near = lane < value.shape[1] // 2
+    return jnp.concatenate([jnp.where(near, value, 0.0), jnp.where(near, 0.0, value)], axis=0)
+
+
+def lower_correction(gram, count):
+    row = lax.broadcasted_iota(jnp.int32, gram.shape, 0)
+    col = lax.rem(lax.broadcasted_iota(jnp.int32, gram.shape, 1), count)
+    return jnp.where(row > col, -gram, jnp.where(row == col, 1.5 - 0.5 * gram, 0.0))
+
+
+def solve_small(gram, rows):
+    count = gram.shape[0]
     half = count // 2
     r = lax.broadcasted_iota(jnp.int32, gram.shape, 0)
     c = lax.broadcasted_iota(jnp.int32, gram.shape, 1)
-    own_pair = jnp.where((r < half) == (c < half), gram, 0.0)
-    first = orthogonal_iteration(pair_ref[...], own_pair, 2)
-    reached = dot_nn(first, gram)
-    kernel = dot_nt(reached, first)
-    second = orthogonal_iteration(start_ref[...], kernel, 1)
-    weights = dot_nn(second, first)
-    projected = dot_nn(second, reached)
-    capacitance = dot_nt(projected, weights)
-    columns = spread_columns(capacitance, 0, rows, 2 * count)
-    total = sum(columns[j][j // 8][j % 8 : j % 8 + 1] for j in range(rows))
-    damping = 0.1 * total / rows + 1e-06
+    lane = lax.broadcasted_iota(jnp.int32, (1, count), 1)
+    diagonal = jnp.sum(jnp.where(r == c, gram, 0.0), axis=0, keepdims=True)
+    trace_lower = jnp.sum(jnp.where(lane < half, diagonal, 0.0), axis=1, keepdims=True)
+    trace_upper = jnp.sum(jnp.where(lane < half, 0.0, diagonal), axis=1, keepdims=True)
+    scale = 1.0 / (trace_lower + trace_upper)
+    own_pair = jnp.where((r < half) == (c < half), gram, 0.0) / jnp.where(lane < half, trace_lower, trace_upper)
+    gram = gram * scale
+
+    moved = dot_nn(start_rows(rows, count, half), own_pair)
+    for step in range(ITERS):
+        inner = dot_nt(moved, apart(moved))
+        onward = dot_nn(moved, own_pair) if step < ITERS - 1 else moved
+        moved = eliminate(spread(inner, 2, rows, count), onward)
+    both = apart(moved)
+    basis = apart(dot_nn(lower_correction(dot_nt(moved, both), rows), both))
+
+    reached = dot_nn(basis, gram)
+    kernel = dot_nt(reached, basis)
+    moved = dot_nn(start_rows(rows, half, half), kernel)
+    for step in range(ITERS - 1):
+        inner = dot_nt(moved, moved)
+        moved = eliminate(spread(inner, 1, rows, half), dot_nn(moved, kernel))
+    inner = dot_nt(moved, moved)
+    onward = dot_nn(moved, jnp.concatenate([reached, basis], axis=1))
+    both = eliminate(spread(inner, 1, rows, 2 * count), onward)
+
+    weights = both[:, count:]
+    joint = dot_nt(jnp.concatenate([both[:, :count], weights], axis=0), weights)
+    energy = spread(joint[:rows], 1, rows, 2 * count)
+    metric = spread(joint[rows:], 1, rows, 2 * count)
     row = lax.broadcasted_iota(jnp.int32, (8, 2 * count), 0)
+    total = jnp.zeros((8, 2 * count), jnp.float32)
     for j in range(rows):
-        columns[j][j // 8] = columns[j][j // 8] + jnp.where(row == j % 8, damping, 0.0)
-    solved = eliminate(columns, jnp.concatenate([projected, weights], axis=1))
+        for b in energy[j]:
+            unit = jnp.where(row == j % 8, 2.0, 0.0) if b == j // 8 else 0.0
+            term = energy[j][b] * (unit - metric[j][b])
+            total = total + (term if b == j // 8 else term + term)
+    damping = 0.1 * jnp.sum(total, axis=0, keepdims=True) / rows + 1e-06 * scale
+    columns = [{b: energy[j][b] + damping * metric[j][b] for b in energy[j]} for j in range(rows)]
+    solved = eliminate(columns, both)
+    return solved[:, :count], solved[:, count:]
+
+
+def combine_kernel(rows, leaf_ref, out_ref, change_ref):
+    leaf = leaf_ref[...]
+    gram = lax.dot_general(leaf, leaf, (((1,), (1,)), ((), ())), preferred_element_type=jnp.float32)
+    projected, weights = solve_small(gram, rows)
     change_ref[...] = lax.dot_general(
-        solved[:, :count], solved[:, count:], (((0,), (0,)), ((), ())), precision=HI, preferred_element_type=jnp.float32
+        projected, weights, (((0,), (0,)), ((), ())), precision=HI, preferred_element_type=jnp.float32
     )
     own = pl.ds(pl.multiple_of(lax.axis_index("grp") * rows, rows), rows)
     change = change_ref[own, :]
@@ -217,16 +271,12 @@
     pieces = pieces.reshape(groups * modules, own, width // splits)
     leaf = lax.all_to_all(pieces, ("grp", "mod"), split_axis=0, concat_axis=0, tiled=True)
     leaf = leaf.reshape(count, width // splits)
-    start = start_basis(2 * rows, rows).T
-    pair = np.zeros((2 * rows, 4 * rows), np.float32)
-    pair[:rows, : 2 * rows] = start
-    pair[rows:, 2 * rows :] = start
     return pl.pallas_call(
         functools.partial(combine_kernel, rows),
         out_shape=jax.ShapeDtypeStruct((1, rows, width), jnp.float32),
         scratch_shapes=[pltpu.VMEM((count, count), jnp.float32)],
         compiler_params=pltpu.CompilerParams(vmem_limit_bytes=32 * 1024 * 1024),
-    )(jnp.asarray(start), jnp.asarray(pair), leaf)
+    )(leaf)
 
 
 def local_features(token_block, live_counts):

time: 33 us -> 31.6 us (0.958)
  Pallas kernels: 7.71 us -> 6.99 us
  local copies, waits for them, and re-layouts: 2.33 us -> 1.82 us
    pallas_call x1, Pallas kernels: 6.27 us -> 5.55 us  [gram_route(): pl.pallas_call(functools.partial(combine_kernel, rows), out_shape=jax.Sha...]
    unnamed x10 -> x6, local copies, waits for them, and re-layouts: 2.14 us -> 1.62 us
where the time goes in v5:
time: 31.6 us; the launch traced here: 31.5 us
  blocking collectives  22.7 us (72%)
  Pallas kernels  6.99 us (22%)
  local copies, waits for them, and re-layouts  1.82 us (6%)
    all_to_all x1, blocking collectives, gram_route(): lax.all_to_all(pieces, ('grp', 'mod'), split_axis=0, concat_axis=0, tiled...  22.7 us
    pallas_call x1, Pallas kernels, gram_route(): pl.pallas_call(functools.partial(combine_kernel, rows), out_shape=jax.Sha...  5.55 us
    unnamed x6, local copies, waits for them, and re-layouts  1.62 us
    pallas_call x1, Pallas kernels, gram_route(): pl.pallas_call(functools.partial(features_kernel, splits), out_shape=jax....  1.44 us

profile of v5, /device:TPU:0, one launch (start us, length us, event | category | flops | bytes accessed | tf_op | source)
XLA Modules:
  0.0 31.5 jit_solution(14794676076750711265)
XLA Ops:
  0.0 0.0 copy-start.2
  0.0 0.0 copy-start.1
  0.0 0.7 %copy-done.2 = s32[8]{0:T(128)S(1)} copy-done((s32[8]{0:T(128)S(1)}, s32[8]{0:T(128)}, u32[]{:S(2)}) %copy-start.2) | copy-done | bytes 56
  0.7 0.0 copy-done.1
  0.7 0.0 copy-start
  0.7 0.9 %copy-done = bf16[2,64,8,128]{3,2,1,0:T(8,128)(2,1)S(1)} copy-done((bf16[2,64,8,128]{3,2,1,0:T(8,128)(2,1)S(1)}, bf16[2,64,8,128]{3,2,1,0:T(8,128)(2,1)}, u32[]{:S(2)}) %copy-start) | copy-done | bytes 262168
  1.6 1.4 %shard_map.37 = bf16[4,8,2,4096]{3,2,1,0:T(2,128)(2,1)S(1)} custom-call(s32[2]{0:T(128)S(1)} %copy-done.1, s32[8]{0:T(128)S(1)} %copy-done.2, bf16[2,512,128]{2,1,0:T(8,128)(2,1)S(1)} %bitcast.3), custom_call_target="tpu_custom_call" | custom-call | tf_op jit(solution)/shard_map/pallas_call | solution.py:260
  3.1 22.7 %all_to_all.5 = bf16[32,2,4096]{2,1,0:T(2,128)(2,1)S(1)} all-to-all(bf16[32,2,4096]{2,1,0:T(2,128)(2,1)S(1)} %bitcast.2), channel_id=1, replica_groups=mesh['grp'=4,'mod'=8] {'grp','mod'}, dimensions={0} | all-to-all | bytes 1048576 | tf_op jit(solution)/shard_map/all_to_all | solution.py:272
  25.7 0.2 reshape.11.leaf_ref
  25.9 5.6 %shard_map.38 = f32[1,16,4096]{2,1,0:T(8,128)} custom-call(bf16[64,4096]{1,0:T(8,128)(2,1)S(1)} %reshape.11.leaf_ref), custom_call_target="tpu_custom_call" | custom-call | tf_op jit(solution)/shard_map/pallas_call | solution.py:274
Async XLA Ops:
  0.0 0.7 %copy-start.2 = (s32[8]{0:T(128)S(1)}, s32[8]{0:T(128)}, u32[]{:S(2)}) copy-start(s32[8]{0:T(128)} %order_ref.1) | copy-start | bytes 100
  0.0 0.7 %copy-start.1 = (s32[2]{0:T(128)S(1)}, s32[2]{0:T(128)}, u32[]{:S(2)}) copy-start(s32[2]{0:T(128)} %lengths_ref.1) | copy-start | bytes 28
  0.7 0.9 %copy-start = (bf16[2,64,8,128]{3,2,1,0:T(8,128)(2,1)S(1)}, bf16[2,64,8,128]{3,2,1,0:T(8,128)(2,1)}, u32[]{:S(2)}) copy-start(bf16[2,64,8,128]{3,2,1,0:T(8,128)(2,1)} %param.3) | copy-start | bytes 786436

commit v6 on v5

--- a/solution.py
+++ b/solution.py
@@ -116,6 +116,7 @@
     parts = [rhs[8 * b : 8 * b + 8] for b in range(count // 8)]
     row = lax.broadcasted_iota(jnp.int32, (8, width), 0)
     diag = [jnp.ones((8, width), jnp.float32) for _ in parts]
+    whole = [functools.reduce(lambda x, j: jnp.where(row == j, columns[8 * k + j][k], x), range(8), d) for k, d in enumerate(diag)]
     for p in range(0, count, 2):
         home, at = divmod(p, 8)
         left, right = columns[p], columns[p + 1]
@@ -140,7 +141,8 @@
         first, second = parts[home][at : at + 1], parts[home][at + 1 : at + 2]
         for k in low:
             parts[k] = parts[k] - (low[k] * first + high[k] * second)
-    return jnp.concatenate([part * lax.rsqrt(d) for part, d in zip(parts, diag)], axis=0)
+    worst = functools.reduce(jnp.minimum, [d / w for d, w in zip(diag, whole)])
+    return jnp.concatenate([part * lax.rsqrt(d) for part, d in zip(parts, diag)], axis=0), worst
 
 
 def apart(value):
@@ -155,7 +157,7 @@
     return jnp.where(row > col, -gram, jnp.where(row == col, 1.5 - 0.5 * gram, 0.0))
 
 
-def solve_small(gram, rows):
+def solve_small(gram, rows, often):
     count = gram.shape[0]
     half = count // 2
     r = lax.broadcasted_iota(jnp.int32, gram.shape, 0)
@@ -169,22 +171,30 @@
     gram = gram * scale
 
     moved = dot_nn(start_rows(rows, count, half), own_pair)
-    for step in range(ITERS):
-        inner = dot_nt(moved, apart(moved))
-        onward = dot_nn(moved, own_pair) if step < ITERS - 1 else moved
-        moved = eliminate(spread(inner, 2, rows, count), onward)
+    if often:
+        for step in range(ITERS - 1):
+            inner = dot_nt(moved, apart(moved))
+            moved, _ = eliminate(spread(inner, 2, rows, count), dot_nn(moved, own_pair))
+    else:
+        moved = dot_nn(moved, dot_nn(own_pair, own_pair))
+    inner = dot_nt(moved, apart(moved))
+    moved, worst_pair = eliminate(spread(inner, 2, rows, count), moved)
     both = apart(moved)
     basis = apart(dot_nn(lower_correction(dot_nt(moved, both), rows), both))
 
     reached = dot_nn(basis, gram)
     kernel = dot_nt(reached, basis)
     moved = dot_nn(start_rows(rows, half, half), kernel)
-    for step in range(ITERS - 1):
-        inner = dot_nt(moved, moved)
-        moved = eliminate(spread(inner, 1, rows, half), dot_nn(moved, kernel))
+    if often:
+        for step in range(ITERS - 1):
+            inner = dot_nt(moved, moved)
+            moved, _ = eliminate(spread(inner, 1, rows, half), dot_nn(moved, kernel))
+    else:
+        moved = dot_nn(moved, dot_nn(kernel, kernel))
     inner = dot_nt(moved, moved)
     onward = dot_nn(moved, jnp.concatenate([reached, basis], axis=1))
-    both = eliminate(spread(inner, 1, rows, 2 * count), onward)
+    both, worst_last = eliminate(spread(inner, 1, rows, 2 * count), onward)
+    enough = jnp.logical_and(jnp.min(worst_pair) > 2e-5, jnp.min(worst_last) > 2e-4)
 
     weights = both[:, count:]
     joint = dot_nt(jnp.concatenate([both[:, :count], weights], axis=0), weights)
@@ -199,23 +209,32 @@
             total = total + (term if b == j // 8 else term + term)
     damping = 0.1 * jnp.sum(total, axis=0, keepdims=True) / rows + 1e-06 * scale
     columns = [{b: energy[j][b] + damping * metric[j][b] for b in energy[j]} for j in range(rows)]
-    solved = eliminate(columns, both)
-    return solved[:, :count], solved[:, count:]
-
-
-def combine_kernel(rows, leaf_ref, out_ref, change_ref):
+    solved, _ = eliminate(columns, both)
+    return solved[:, :count], solved[:, count:], enough
+
+
+def combine_kernel(rows, leaf_ref, out_ref, gram_ref, change_ref):
     leaf = leaf_ref[...]
-    gram = lax.dot_general(leaf, leaf, (((1,), (1,)), ((), ())), preferred_element_type=jnp.float32)
-    projected, weights = solve_small(gram, rows)
-    change_ref[...] = lax.dot_general(
-        projected, weights, (((0,), (0,)), ((), ())), precision=HI, preferred_element_type=jnp.float32
-    )
+    gram_ref[...] = lax.dot_general(leaf, leaf, (((1,), (1,)), ((), ())), preferred_element_type=jnp.float32)
     own = pl.ds(pl.multiple_of(lax.axis_index("grp") * rows, rows), rows)
-    change = change_ref[own, :]
-    top = change.astype(jnp.bfloat16)
-    rest = (change - top.astype(jnp.float32)).astype(jnp.bfloat16)
-    moved = jnp.dot(top, leaf, preferred_element_type=jnp.float32) + jnp.dot(rest, leaf, preferred_element_type=jnp.float32)
-    out_ref[0] = leaf_ref[own, :].astype(jnp.float32) - moved
+
+    def finish(often):
+        projected, weights, enough = solve_small(gram_ref[...], rows, often)
+        change_ref[...] = lax.dot_general(
+            projected, weights, (((0,), (0,)), ((), ())), precision=HI, preferred_element_type=jnp.float32
+        )
+        change = change_ref[own, :]
+        top = change.astype(jnp.bfloat16)
+        rest = (change - top.astype(jnp.float32)).astype(jnp.bfloat16)
+        moved = jnp.dot(jnp.concatenate([top, rest], axis=0), leaf_ref[...], preferred_element_type=jnp.float32)
+        out_ref[0] = leaf_ref[own, :].astype(jnp.float32) - (moved[:rows] + moved[rows:])
+        return enough
+
+    enough = finish(False)
+
+    @pl.when(jnp.logical_not(enough))
+    def _():
+        finish(True)
 
 
 def features_kernel(splits, lengths_ref, order_ref, tokens_ref, out_ref, held_ref):
@@ -274,7 +293,7 @@
     return pl.pallas_call(
         functools.partial(combine_kernel, rows),
         out_shape=jax.ShapeDtypeStruct((1, rows, width), jnp.float32),
-        scratch_shapes=[pltpu.VMEM((count, count), jnp.float32)],
+        scratch_shapes=[pltpu.VMEM((count, count), jnp.float32)] * 2,
         compiler_params=pltpu.CompilerParams(vmem_limit_bytes=32 * 1024 * 1024),
     )(leaf)
 

time: 31.6 us -> 34.9 us (1.10)
  Pallas kernels: 6.99 us -> 10.2 us
    pallas_call x1, Pallas kernels: 5.55 us -> 8.78 us  [gram_route(): pl.pallas_call(functools.partial(combine_kernel, rows), out_shape=jax.Sha...]
where the time goes in v6:
time: 34.9 us; the launch traced here: 34.7 us
  blocking collectives  22.7 us (65%)
  Pallas kernels  10.2 us (29%)
  local copies, waits for them, and re-layouts  1.82 us (5%)
    all_to_all x1, blocking collectives, gram_route(): lax.all_to_all(pieces, ('grp', 'mod'), split_axis=0, concat_axis=0, tiled...  22.7 us
    pallas_call x1, Pallas kernels, gram_route(): pl.pallas_call(functools.partial(combine_kernel, rows), out_shape=jax.Sha...  8.78 us
    unnamed x6, local copies, waits for them, and re-layouts  1.62 us
    pallas_call x1, Pallas kernels, gram_route(): pl.pallas_call(functools.partial(features_kernel, splits), out_shape=jax....  1.44 us

profile of v6, /device:TPU:0, one launch (start us, length us, event | category | flops | bytes accessed | tf_op | source)
XLA Modules:
  0.0 34.7 jit_solution(17255961285957204431)
XLA Ops:
  0.0 0.0 copy-start.2
  0.0 0.0 copy-start.1
  0.0 0.7 %copy-done.2 = s32[8]{0:T(128)S(1)} copy-done((s32[8]{0:T(128)S(1)}, s32[8]{0:T(128)}, u32[]{:S(2)}) %copy-start.2) | copy-done | bytes 56
  0.7 0.0 copy-done.1
  0.7 0.0 copy-start
  0.7 0.9 %copy-done = bf16[2,64,8,128]{3,2,1,0:T(8,128)(2,1)S(1)} copy-done((bf16[2,64,8,128]{3,2,1,0:T(8,128)(2,1)S(1)}, bf16[2,64,8,128]{3,2,1,0:T(8,128)(2,1)}, u32[]{:S(2)}) %copy-start) | copy-done | bytes 262168
  1.6 1.4 %shard_map.37 = bf16[4,8,2,4096]{3,2,1,0:T(2,128)(2,1)S(1)} custom-call(s32[2]{0:T(128)S(1)} %copy-done.1, s32[8]{0:T(128)S(1)} %copy-done.2, bf16[2,512,128]{2,1,0:T(8,128)(2,1)S(1)} %bitcast.3), custom_call_target="tpu_custom_call" | custom-call | tf_op jit(solution)/shard_map/pallas_call | solution.py:279
  3.1 22.7 %all_to_all.5 = bf16[32,2,4096]{2,1,0:T(2,128)(2,1)S(1)} all-to-all(bf16[32,2,4096]{2,1,0:T(2,128)(2,1)S(1)} %bitcast.2), channel_id=1, replica_groups=mesh['grp'=4,'mod'=8] {'grp','mod'}, dimensions={0} | all-to-all | bytes 1048576 | tf_op jit(solution)/shard_map/all_to_all | solution.py:291
  25.7 0.2 reshape.11.leaf_ref
  25.9 8.8 %shard_map.38 = f32[1,16,4096]{2,1,0:T(8,128)} custom-call(bf16[64,4096]{1,0:T(8,128)(2,1)S(1)} %reshape.11.leaf_ref), custom_call_target="tpu_custom_call" | custom-call | tf_op jit(solution)/shard_map/pallas_call | solution.py:293
Async XLA Ops:
  0.0 0.7 %copy-start.2 = (s32[8]{0:T(128)S(1)}, s32[8]{0:T(128)}, u32[]{:S(2)}) copy-start(s32[8]{0:T(128)} %order_ref.1) | copy-start | bytes 100
  0.0 0.7 %copy-start.1 = (s32[2]{0:T(128)S(1)}, s32[2]{0:T(128)}, u32[]{:S(2)}) copy-start(s32[2]{0:T(128)} %lengths_ref.1) | copy-start | bytes 28
  0.7 0.9 %copy-start = (bf16[2,64,8,128]{3,2,1,0:T(8,128)(2,1)S(1)}, bf16[2,64,8,128]{3,2,1,0:T(8,128)(2,1)}, u32[]{:S(2)}) copy-start(bf16[2,64,8,128]{3,2,1,0:T(8,128)(2,1)} %param.3) | copy-start | bytes 786436

commit v7 on v6

--- a/solution.py
+++ b/solution.py
@@ -11,6 +11,7 @@
 
 ITERS = 3
 HI = lax.Precision.HIGHEST
+VMEM_BYTES = 48 * 1024 * 1024
 
 
 def partner(value, axis, bit):
@@ -213,10 +214,11 @@
     return solved[:, :count], solved[:, count:], enough
 
 
-def combine_kernel(rows, leaf_ref, out_ref, gram_ref, change_ref):
+def combine_kernel(rows, pieces, leaf_ref, out_ref, gram_ref, change_ref, held_ref, sems):
     leaf = leaf_ref[...]
     gram_ref[...] = lax.dot_general(leaf, leaf, (((1,), (1,)), ((), ())), preferred_element_type=jnp.float32)
     own = pl.ds(pl.multiple_of(lax.axis_index("grp") * rows, rows), rows)
+    span = leaf_ref.shape[1] // pieces
 
     def finish(often):
         projected, weights, enough = solve_small(gram_ref[...], rows, often)
@@ -226,8 +228,16 @@
         change = change_ref[own, :]
         top = change.astype(jnp.bfloat16)
         rest = (change - top.astype(jnp.float32)).astype(jnp.bfloat16)
-        moved = jnp.dot(jnp.concatenate([top, rest], axis=0), leaf_ref[...], preferred_element_type=jnp.float32)
-        out_ref[0] = leaf_ref[own, :].astype(jnp.float32) - (moved[:rows] + moved[rows:])
+        both = jnp.concatenate([top, rest], axis=0)
+        copies = []
+        for k in range(pieces):
+            part = slice(k * span, (k + 1) * span)
+            moved = jnp.dot(both, leaf_ref[:, part], preferred_element_type=jnp.float32)
+            held_ref[:, part] = leaf_ref[own, part].astype(jnp.float32) - (moved[:rows] + moved[rows:])
+            copies.append(pltpu.make_async_copy(held_ref.at[:, part], out_ref.at[0, :, part], sems.at[k]))
+            copies[-1].start()
+        for copy in copies:
+            copy.wait()
         return enough
 
     enough = finish(False)
@@ -237,64 +247,86 @@
         finish(True)
 
 
-def features_kernel(splits, lengths_ref, order_ref, tokens_ref, out_ref, held_ref):
+def features_kernel(lengths_hbm, order_hbm, tokens_hbm, out_ref, lengths_ref, order_ref, tokens_ref, grads_ref, held_ref, sems):
     examples, depth, full = tokens_ref.shape
+    groups, modules, _, width = out_ref.shape
     half = full // 2
-    modules = order_ref.shape[0]
-    chunks = half * half // full
-    position = lax.broadcasted_iota(jnp.int32, (modules, depth), 1)
-    module = lax.broadcasted_iota(jnp.int32, (modules, depth), 0)
-    mine = lax.rem(position, modules) == module
+    chunks = width // full
+    pairs = chunks * examples
+    copies = [
+        pltpu.make_async_copy(lengths_hbm, lengths_ref, sems.at[0]),
+        pltpu.make_async_copy(order_hbm, order_ref, sems.at[1]),
+    ]
+    for e in range(examples):
+        copies.append(pltpu.make_async_copy(tokens_hbm.at[e], tokens_ref.at[e], sems.at[2 + e]))
+    for copy in copies:
+        copy.start()
+    position = lax.broadcasted_iota(jnp.int32, (chunks, depth), 1)
+    module = lax.rem(position, modules)
     lane = lax.broadcasted_iota(jnp.int32, (depth, full), 1)
+    copies[0].wait()
+    copies[1].wait()
     for e in range(examples):
+        copies[2 + e].wait()
         block = tokens_ref[e].astype(jnp.float32)
-        grads = block.T[half:]
-        live = jnp.logical_and(mine, position < lengths_ref[e] * modules)
-        rows = []
-        for o in range(half):
-            rows.append(jnp.where(live, grads[o : o + 1], 0.0).astype(jnp.bfloat16))
-        even = jnp.concatenate(rows[0::2], axis=0)
-        odd = jnp.concatenate(rows[1::2], axis=0)
         left = jnp.where(lane < half, block, 0.0).astype(jnp.bfloat16)
         right = jnp.where(lane < half, 0.0, pltpu.roll(block, half, 1)).astype(jnp.bfloat16)
-        flat = jnp.dot(even, left, preferred_element_type=jnp.float32) + jnp.dot(odd, right, preferred_element_type=jnp.float32)
+        grads = block.T[half:]
+        for k in range(depth // full):
+            grads_ref[k] = grads[:, k * full : (k + 1) * full]
+        live = position < lengths_ref[e] * modules
+        flat = jnp.zeros((modules * chunks, full), jnp.float32)
+        for odd, side in ((0, left), (1, right)):
+            every = pl.ds(odd, chunks, stride=2)
+            grads = jnp.concatenate([grads_ref[k, every, :] for k in range(depth // full)], axis=1)
+            grads = jnp.where(live, grads, 0.0)
+            apiece = [jnp.where(module == q, grads, 0.0).astype(jnp.bfloat16) for q in range(modules)]
+            flat = flat + jnp.dot(jnp.concatenate(apiece, axis=0), side, preferred_element_type=jnp.float32)
+        held_ref[pl.ds(e, modules * chunks, stride=examples), :] = flat
+    for slot in range(modules):
+        first = pl.multiple_of(order_ref[slot] * pairs, pairs)
         for c in range(chunks):
-            held_ref[pl.ds(c * modules * examples + e, modules, stride=examples), :] = flat[c * modules : (c + 1) * modules]
-    groups = out_ref.shape[0]
-    span = chunks // splits
-    for slot in range(modules):
-        first = order_ref[slot] * examples
-        for c in range(chunks):
-            pair = held_ref[pl.ds(c * modules * examples + first, examples), :].astype(jnp.bfloat16)
-            for g in range(c // span, groups, splits):
-                out_ref[g, slot, :, (c % span) * full : (c % span + 1) * full] = pair
-
-
-def gram_route(tokens, lengths, module_order, splits=1):
+            piece = held_ref[pl.ds(first + c * examples, examples), :].astype(jnp.bfloat16)
+            for g in range(groups):
+                out_ref[g, slot, :, c * full : (c + 1) * full] = piece
+
+
+def gram_route(tokens, lengths, module_order):
     groups, owners = lax.axis_size("grp"), lax.axis_size("mod")
     own, slots, modules, full = tokens.shape
     width = (full // 2) ** 2
     rows = owners * own
     count = groups * rows
-    pieces = pl.pallas_call(
-        functools.partial(features_kernel, splits),
-        out_shape=jax.ShapeDtypeStruct((groups, modules, own, width // splits), jnp.bfloat16),
-        in_specs=[
-            pl.BlockSpec(memory_space=pltpu.SMEM),
-            pl.BlockSpec(memory_space=pltpu.SMEM),
-            pl.BlockSpec(memory_space=pltpu.VMEM),
+    chunks = width // full
+    messages = pl.pallas_call(
+        features_kernel,
+        out_shape=jax.ShapeDtypeStruct((groups, modules, own, width), jnp.bfloat16),
+        in_specs=[pl.BlockSpec(memory_space=pltpu.HBM)] * 3,
+        scratch_shapes=[
+            pltpu.SMEM(lengths.shape, jnp.int32),
+            pltpu.SMEM(module_order.shape, jnp.int32),
+            pltpu.VMEM((own, slots * modules, full), jnp.bfloat16),
+            pltpu.VMEM((slots * modules // full, full // 2, full), jnp.float32),
+            pltpu.VMEM((modules * chunks * own, full), jnp.float32),
+            pltpu.SemaphoreType.DMA((2 + own,)),
         ],
-        scratch_shapes=[pltpu.VMEM((own * modules * width // full, full), jnp.float32)],
-        compiler_params=pltpu.CompilerParams(vmem_limit_bytes=32 * 1024 * 1024),
+        compiler_params=pltpu.CompilerParams(vmem_limit_bytes=VMEM_BYTES),
     )(lengths, module_order, tokens.reshape(own, slots * modules, full))
-    pieces = pieces.reshape(groups * modules, own, width // splits)
-    leaf = lax.all_to_all(pieces, ("grp", "mod"), split_axis=0, concat_axis=0, tiled=True)
-    leaf = leaf.reshape(count, width // splits)
+    messages = messages.reshape(groups * modules, own, width)
+    leaf = lax.all_to_all(messages, ("grp", "mod"), split_axis=0, concat_axis=0, tiled=True)
+    leaf = leaf.reshape(count, width)
+    pieces = 4
     return pl.pallas_call(
-        functools.partial(combine_kernel, rows),
+        functools.partial(combine_kernel, rows, pieces),
         out_shape=jax.ShapeDtypeStruct((1, rows, width), jnp.float32),
-        scratch_shapes=[pltpu.VMEM((count, count), jnp.float32)] * 2,
-        compiler_params=pltpu.CompilerParams(vmem_limit_bytes=32 * 1024 * 1024),
+        out_specs=pl.BlockSpec(memory_space=pl.ANY),
+        scratch_shapes=[
+            pltpu.VMEM((count, count), jnp.float32),
+            pltpu.VMEM((count, count), jnp.float32),
+            pltpu.VMEM((rows, width), jnp.float32),
+            pltpu.SemaphoreType.DMA((pieces,)),
+        ],
+        compiler_params=pltpu.CompilerParams(vmem_limit_bytes=VMEM_BYTES),
     )(leaf)
 
 

time: 34.9 us -> 35.7 us (1.023)
  Pallas kernels: 10.2 us -> 11.1 us
    pallas_call x2, Pallas kernels: 10.2 us -> 11.1 us  [the longest x1 9.37 us: gram_route(): pl.pallas_call(functools.partial(combine_kernel, rows, pieces), out_shape...]
where the time goes in v7:
time: 35.7 us; the launch traced here: 35.6 us
  blocking collectives  22.7 us (64%)
  Pallas kernels  11.1 us (31%)
  local copies, waits for them, and re-layouts  1.82 us (5%)
    all_to_all x1, blocking collectives, gram_route(): lax.all_to_all(messages, ('grp', 'mod'), split_axis=0, concat_axis=0, til...  22.7 us
    pallas_call x1, Pallas kernels, gram_route(): pl.pallas_call(functools.partial(combine_kernel, rows, pieces), out_shape...  9.37 us
    pallas_call x1, Pallas kernels, gram_route(): pl.pallas_call(features_kernel, out_shape=jax.ShapeDtypeStruct((groups, m...  1.7 us
    unnamed x6, local copies, waits for them, and re-layouts  1.62 us

profile of v7, /device:TPU:0, one launch (start us, length us, event | category | flops | bytes accessed | tf_op | source)
XLA Modules:
  0.0 35.6 jit_solution(1999260881027977247)
XLA Ops:
  0.0 0.0 copy-start.2
  0.0 0.0 copy-start.1
  0.0 0.7 %copy-done.2 = s32[8]{0:T(128)S(1)} copy-done((s32[8]{0:T(128)S(1)}, s32[8]{0:T(128)}, u32[]{:S(2)}) %copy-start.2) | copy-done | bytes 56
  0.7 0.0 copy-done.1
  0.7 0.0 copy-start
  0.7 0.9 %copy-done = bf16[2,64,8,128]{3,2,1,0:T(8,128)(2,1)S(1)} copy-done((bf16[2,64,8,128]{3,2,1,0:T(8,128)(2,1)S(1)}, bf16[2,64,8,128]{3,2,1,0:T(8,128)(2,1)}, u32[]{:S(2)}) %copy-start) | copy-done | bytes 262168
  1.6 1.7 %shard_map.37 = bf16[4,8,2,4096]{3,2,1,0:T(2,128)(2,1)S(1)} custom-call(s32[2]{0:T(128)S(1)} %copy-done.1, s32[8]{0:T(128)S(1)} %copy-done.2, bf16[2,512,128]{2,1,0:T(8,128)(2,1)S(1)} %bitcast.3), custom_call_target="tpu_custom_call" | custom-call | tf_op jit(solution)/shard_map/pallas_call | solution.py:301
  3.3 22.7 %all_to_all.5 = bf16[32,2,4096]{2,1,0:T(2,128)(2,1)S(1)} all-to-all(bf16[32,2,4096]{2,1,0:T(2,128)(2,1)S(1)} %bitcast.2), channel_id=1, replica_groups=mesh['grp'=4,'mod'=8] {'grp','mod'}, dimensions={0} | all-to-all | bytes 1048576 | tf_op jit(solution)/shard_map/all_to_all | solution.py:316
  26.0 0.2 reshape.11.leaf_ref
  26.2 9.4 %shard_map.38 = f32[1,16,4096]{2,1,0:T(8,128)} custom-call(bf16[64,4096]{1,0:T(8,128)(2,1)S(1)} %reshape.11.leaf_ref), custom_call_target="tpu_custom_call" | custom-call | tf_op jit(solution)/shard_map/pallas_call | solution.py:319
Async XLA Ops:
  0.0 0.7 %copy-start.2 = (s32[8]{0:T(128)S(1)}, s32[8]{0:T(128)}, u32[]{:S(2)}) copy-start(s32[8]{0:T(128)} %order_hbm.1) | copy-start | bytes 100
  0.0 0.7 %copy-start.1 = (s32[2]{0:T(128)S(1)}, s32[2]{0:T(128)}, u32[]{:S(2)}) copy-start(s32[2]{0:T(128)} %lengths_hbm.1) | copy-start | bytes 28
  0.7 0.9 %copy-start = (bf16[2,64,8,128]{3,2,1,0:T(8,128)(2,1)S(1)}, bf16[2,64,8,128]{3,2,1,0:T(8,128)(2,1)}, u32[]{:S(2)}) copy-start(bf16[2,64,8,128]{3,2,1,0:T(8,128)(2,1)} %param.3) | copy-start | bytes 786436

commit v8 on v7

--- a/solution.py
+++ b/solution.py
@@ -214,11 +214,10 @@
     return solved[:, :count], solved[:, count:], enough
 
 
-def combine_kernel(rows, pieces, leaf_ref, out_ref, gram_ref, change_ref, held_ref, sems):
+def combine_kernel(rows, leaf_ref, out_ref, gram_ref, change_ref):
     leaf = leaf_ref[...]
     gram_ref[...] = lax.dot_general(leaf, leaf, (((1,), (1,)), ((), ())), preferred_element_type=jnp.float32)
     own = pl.ds(pl.multiple_of(lax.axis_index("grp") * rows, rows), rows)
-    span = leaf_ref.shape[1] // pieces
 
     def finish(often):
         projected, weights, enough = solve_small(gram_ref[...], rows, often)
@@ -228,16 +227,8 @@
         change = change_ref[own, :]
         top = change.astype(jnp.bfloat16)
         rest = (change - top.astype(jnp.float32)).astype(jnp.bfloat16)
-        both = jnp.concatenate([top, rest], axis=0)
-        copies = []
-        for k in range(pieces):
-            part = slice(k * span, (k + 1) * span)
-            moved = jnp.dot(both, leaf_ref[:, part], preferred_element_type=jnp.float32)
-            held_ref[:, part] = leaf_ref[own, part].astype(jnp.float32) - (moved[:rows] + moved[rows:])
-            copies.append(pltpu.make_async_copy(held_ref.at[:, part], out_ref.at[0, :, part], sems.at[k]))
-            copies[-1].start()
-        for copy in copies:
-            copy.wait()
+        moved = jnp.dot(jnp.concatenate([top, rest], axis=0), leaf_ref[...], preferred_element_type=jnp.float32)
+        out_ref[0] = leaf_ref[own, :].astype(jnp.float32) - (moved[:rows] + moved[rows:])
         return enough
 
     enough = finish(False)
@@ -247,27 +238,15 @@
         finish(True)
 
 
-def features_kernel(lengths_hbm, order_hbm, tokens_hbm, out_ref, lengths_ref, order_ref, tokens_ref, grads_ref, held_ref, sems):
+def features_kernel(lengths_ref, order_ref, tokens_ref, out_ref, grads_ref, held_ref):
     examples, depth, full = tokens_ref.shape
-    groups, modules, _, width = out_ref.shape
+    groups, modules, pairs, _ = out_ref.shape
     half = full // 2
-    chunks = width // full
-    pairs = chunks * examples
-    copies = [
-        pltpu.make_async_copy(lengths_hbm, lengths_ref, sems.at[0]),
-        pltpu.make_async_copy(order_hbm, order_ref, sems.at[1]),
-    ]
-    for e in range(examples):
-        copies.append(pltpu.make_async_copy(tokens_hbm.at[e], tokens_ref.at[e], sems.at[2 + e]))
-    for copy in copies:
-        copy.start()
+    chunks = pairs // examples
     position = lax.broadcasted_iota(jnp.int32, (chunks, depth), 1)
     module = lax.rem(position, modules)
     lane = lax.broadcasted_iota(jnp.int32, (depth, full), 1)
-    copies[0].wait()
-    copies[1].wait()
     for e in range(examples):
-        copies[2 + e].wait()
         block = tokens_ref[e].astype(jnp.float32)
         left = jnp.where(lane < half, block, 0.0).astype(jnp.bfloat16)
         right = jnp.where(lane < half, 0.0, pltpu.roll(block, half, 1)).astype(jnp.bfloat16)
@@ -285,10 +264,9 @@
         held_ref[pl.ds(e, modules * chunks, stride=examples), :] = flat
     for slot in range(modules):
         first = pl.multiple_of(order_ref[slot] * pairs, pairs)
-        for c in range(chunks):
-            piece = held_ref[pl.ds(first + c * examples, examples), :].astype(jnp.bfloat16)
-            for g in range(groups):
-                out_ref[g, slot, :, c * full : (c + 1) * full] = piece
+        message = held_ref[pl.ds(first, pairs), :].astype(jnp.bfloat16)
+        for g in range(groups):
+            out_ref[g, slot] = message
 
 
 def gram_route(tokens, lengths, module_order):
@@ -300,32 +278,21 @@
     chunks = width // full
     messages = pl.pallas_call(
         features_kernel,
-        out_shape=jax.ShapeDtypeStruct((groups, modules, own, width), jnp.bfloat16),
-        in_specs=[pl.BlockSpec(memory_space=pltpu.HBM)] * 3,
+        out_shape=jax.ShapeDtypeStruct((groups, modules, chunks * own, full), jnp.bfloat16),
+        in_specs=[pl.BlockSpec(memory_space=space) for space in (pltpu.SMEM, pltpu.SMEM, pltpu.VMEM)],
         scratch_shapes=[
-            pltpu.SMEM(lengths.shape, jnp.int32),
-            pltpu.SMEM(module_order.shape, jnp.int32),
-            pltpu.VMEM((own, slots * modules, full), jnp.bfloat16),
             pltpu.VMEM((slots * modules // full, full // 2, full), jnp.float32),
             pltpu.VMEM((modules * chunks * own, full), jnp.float32),
-            pltpu.SemaphoreType.DMA((2 + own,)),
         ],
         compiler_params=pltpu.CompilerParams(vmem_limit_bytes=VMEM_BYTES),
     )(lengths, module_order, tokens.reshape(own, slots * modules, full))
-    messages = messages.reshape(groups * modules, own, width)
+    messages = messages.reshape(groups * modules, chunks, own, full).transpose(0, 2, 1, 3).reshape(groups * modules, own, width)
     leaf = lax.all_to_all(messages, ("grp", "mod"), split_axis=0, concat_axis=0, tiled=True)
     leaf = leaf.reshape(count, width)
-    pieces = 4
     return pl.pallas_call(
-        functools.partial(combine_kernel, rows, pieces),
+        functools.partial(combine_kernel, rows),
         out_shape=jax.ShapeDtypeStruct((1, rows, width), jnp.float32),
-        out_specs=pl.BlockSpec(memory_space=pl.ANY),
-        scratch_shapes=[
-            pltpu.VMEM((count, count), jnp.float32),
-            pltpu.VMEM((count, count), jnp.float32),
-            pltpu.VMEM((rows, width), jnp.float32),
-            pltpu.SemaphoreType.DMA((pieces,)),
-        ],
+        scratch_shapes=[pltpu.VMEM((count, count), jnp.float32)] * 2,
         compiler_params=pltpu.CompilerParams(vmem_limit_bytes=VMEM_BYTES),
     )(leaf)
 

time: 35.7 us -> 34.6 us (0.969)
  Pallas kernels: 11.1 us -> 9.93 us
    pallas_call x1, Pallas kernels: 9.37 us -> 8.78 us  [gram_route(): pl.pallas_call(functools.partial(combine_kernel, rows), out_shape=jax.Sha...]
    pallas_call x1, Pallas kernels: 1.7 us -> 1.15 us  [gram_route(): pl.pallas_call(features_kernel, out_shape=jax.ShapeDtypeStruct((groups, m...]
where the time goes in v8:
time: 34.6 us; the launch traced here: 34.4 us
  blocking collectives  22.6 us (65%)
  Pallas kernels  9.93 us (29%)
  local copies, waits for them, and re-layouts  1.82 us (5%)
    all_to_all x1, blocking collectives, gram_route(): lax.all_to_all(messages, ('grp', 'mod'), split_axis=0, concat_axis=0, til...  22.6 us
    pallas_call x1, Pallas kernels, gram_route(): pl.pallas_call(functools.partial(combine_kernel, rows), out_shape=jax.Sha...  8.78 us
    unnamed x6, local copies, waits for them, and re-layouts  1.62 us
    pallas_call x1, Pallas kernels, gram_route(): pl.pallas_call(features_kernel, out_shape=jax.ShapeDtypeStruct((groups, m...  1.15 us

profile of v8, /device:TPU:0, one launch (start us, length us, event | category | flops | bytes accessed | tf_op | source)
XLA Modules:
  0.0 34.4 jit_solution(12304063036239849271)
XLA Ops:
  0.0 0.0 copy-start.2
  0.0 0.0 copy-start.1
  0.0 0.7 %copy-done.2 = s32[8]{0:T(128)S(1)} copy-done((s32[8]{0:T(128)S(1)}, s32[8]{0:T(128)}, u32[]{:S(2)}) %copy-start.2) | copy-done | bytes 56
  0.7 0.0 copy-done.1
  0.7 0.0 copy-start
  0.7 0.9 %copy-done = bf16[2,64,8,128]{3,2,1,0:T(8,128)(2,1)S(1)} copy-done((bf16[2,64,8,128]{3,2,1,0:T(8,128)(2,1)S(1)}, bf16[2,64,8,128]{3,2,1,0:T(8,128)(2,1)}, u32[]{:S(2)}) %copy-start) | copy-done | bytes 262168
  1.6 1.1 %shard_map.37 = bf16[4,8,64,128]{3,2,1,0:T(8,128)(2,1)S(1)} custom-call(s32[2]{0:T(128)S(1)} %copy-done.1, s32[8]{0:T(128)S(1)} %copy-done.2, bf16[2,512,128]{2,1,0:T(8,128)(2,1)S(1)} %bitcast.7), custom_call_target="tpu_custom_call" | custom-call | tf_op jit(solution)/shard_map/pallas_call | solution.py:279
  2.8 22.6 %all_to_all.5 = bf16[32,2,4096]{2,1,0:T(2,128)(2,1)S(1)} all-to-all(bf16[32,2,4096]{2,1,0:T(2,128)(2,1)S(1)} %bitcast.6), channel_id=1, replica_groups=mesh['grp'=4,'mod'=8] {'grp','mod'}, dimensions={0} | all-to-all | bytes 1048576 | tf_op jit(solution)/shard_map/all_to_all | solution.py:290
  25.4 0.2 reshape.15.leaf_ref
  25.6 8.8 %shard_map.38 = f32[1,16,4096]{2,1,0:T(8,128)} custom-call(bf16[64,4096]{1,0:T(8,128)(2,1)S(1)} %reshape.15.leaf_ref), custom_call_target="tpu_custom_call" | custom-call | tf_op jit(solution)/shard_map/pallas_call | solution.py:292
Async XLA Ops:
  0.0 0.7 %copy-start.2 = (s32[8]{0:T(128)S(1)}, s32[8]{0:T(128)}, u32[]{:S(2)}) copy-start(s32[8]{0:T(128)} %order_ref.1) | copy-start | bytes 100
  0.0 0.7 %copy-start.1 = (s32[2]{0:T(128)S(1)}, s32[2]{0:T(128)}, u32[]{:S(2)}) copy-start(s32[2]{0:T(128)} %lengths_ref.1) | copy-start | bytes 28
  0.7 0.9 %copy-start = (bf16[2,64,8,128]{3,2,1,0:T(8,128)(2,1)S(1)}, bf16[2,64,8,128]{3,2,1,0:T(8,128)(2,1)}, u32[]{:S(2)}) copy-start(bf16[2,64,8,128]{3,2,1,0:T(8,128)(2,1)} %param.3) | copy-start | bytes 786436

commit v9 on v8

--- a/solution.py
+++ b/solution.py
@@ -152,12 +152,6 @@
     return jnp.concatenate([jnp.where(near, value, 0.0), jnp.where(near, 0.0, value)], axis=0)
 
 
-def lower_correction(gram, count):
-    row = lax.broadcasted_iota(jnp.int32, gram.shape, 0)
-    col = lax.rem(lax.broadcasted_iota(jnp.int32, gram.shape, 1), count)
-    return jnp.where(row > col, -gram, jnp.where(row == col, 1.5 - 0.5 * gram, 0.0))
-
-
 def solve_small(gram, rows, often):
     count = gram.shape[0]
     half = count // 2
@@ -168,47 +162,51 @@
     trace_lower = jnp.sum(jnp.where(lane < half, diagonal, 0.0), axis=1, keepdims=True)
     trace_upper = jnp.sum(jnp.where(lane < half, 0.0, diagonal), axis=1, keepdims=True)
     scale = 1.0 / (trace_lower + trace_upper)
-    own_pair = jnp.where((r < half) == (c < half), gram, 0.0) / jnp.where(lane < half, trace_lower, trace_upper)
+    pair_scale = 1.0 / jnp.where(lane < half, trace_lower, trace_upper)
+    own_pair = jnp.where((r < half) == (c < half), gram, 0.0)
+
+    moved = dot_nn(start_rows(rows, count, half), own_pair) * pair_scale
+    own_pair = own_pair * pair_scale
+    smallest = []
+    if not often:
+        moved = dot_nn(moved, own_pair)
+    for onward_too in (True, True, False, False) if often else (True, False):
+        inner = dot_nt(moved, apart(moved))
+        onward = dot_nn(moved, own_pair) if onward_too else moved
+        moved, worst = eliminate(spread(inner, 2, rows, count), onward)
+        smallest.append(jnp.min(worst))
+    basis = apart(moved)
+
     gram = gram * scale
-
-    moved = dot_nn(start_rows(rows, count, half), own_pair)
-    if often:
-        for step in range(ITERS - 1):
-            inner = dot_nt(moved, apart(moved))
-            moved, _ = eliminate(spread(inner, 2, rows, count), dot_nn(moved, own_pair))
-    else:
-        moved = dot_nn(moved, dot_nn(own_pair, own_pair))
-    inner = dot_nt(moved, apart(moved))
-    moved, worst_pair = eliminate(spread(inner, 2, rows, count), moved)
-    both = apart(moved)
-    basis = apart(dot_nn(lower_correction(dot_nt(moved, both), rows), both))
-
     reached = dot_nn(basis, gram)
     kernel = dot_nt(reached, basis)
     moved = dot_nn(start_rows(rows, half, half), kernel)
     if often:
-        for step in range(ITERS - 1):
+        for onward_too in (True, True, False):
             inner = dot_nt(moved, moved)
-            moved, _ = eliminate(spread(inner, 1, rows, half), dot_nn(moved, kernel))
+            onward = dot_nn(moved, kernel) if onward_too else moved
+            moved, _ = eliminate(spread(inner, 1, rows, half), onward)
     else:
         moved = dot_nn(moved, dot_nn(kernel, kernel))
     inner = dot_nt(moved, moved)
     onward = dot_nn(moved, jnp.concatenate([reached, basis], axis=1))
-    both, worst_last = eliminate(spread(inner, 1, rows, 2 * count), onward)
-    enough = jnp.logical_and(jnp.min(worst_pair) > 2e-5, jnp.min(worst_last) > 2e-4)
+    both, worst = eliminate(spread(inner, 1, rows, 2 * count), onward)
+    smallest.append(jnp.min(worst))
+    enough = jnp.logical_and(jnp.logical_and(smallest[0] > 1e-4, smallest[1] > 1e-2), smallest[-1] > 3e-4)
 
     weights = both[:, count:]
+    row = lax.broadcasted_iota(jnp.int32, (8, 2 * count), 0)
     joint = dot_nt(jnp.concatenate([both[:, :count], weights], axis=0), weights)
     energy = spread(joint[:rows], 1, rows, 2 * count)
     metric = spread(joint[rows:], 1, rows, 2 * count)
-    row = lax.broadcasted_iota(jnp.int32, (8, 2 * count), 0)
     total = jnp.zeros((8, 2 * count), jnp.float32)
     for j in range(rows):
         for b in energy[j]:
             unit = jnp.where(row == j % 8, 2.0, 0.0) if b == j // 8 else 0.0
             term = energy[j][b] * (unit - metric[j][b])
             total = total + (term if b == j // 8 else term + term)
-    damping = 0.1 * jnp.sum(total, axis=0, keepdims=True) / rows + 1e-06 * scale
+    total = jnp.sum(total, axis=0, keepdims=True)
+    damping = 0.1 * total / rows + 1e-06 * scale
     columns = [{b: energy[j][b] + damping * metric[j][b] for b in energy[j]} for j in range(rows)]
     solved, _ = eliminate(columns, both)
     return solved[:, :count], solved[:, count:], enough

time: 34.6 us -> 34.8 us (level)
  no operation moved by 1% of the time
where the time goes in v9:
time: 34.8 us; the launch traced here: 34.7 us
  blocking collectives  22.6 us (65%)
  Pallas kernels  10.2 us (29%)
  local copies, waits for them, and re-layouts  1.82 us (5%)
    all_to_all x1, blocking collectives, gram_route(): lax.all_to_all(messages, ('grp', 'mod'), split_axis=0, concat_axis=0, til...  22.6 us
    pallas_call x1, Pallas kernels, gram_route(): pl.pallas_call(functools.partial(combine_kernel, rows), out_shape=jax.Sha...  9.02 us
    unnamed x6, local copies, waits for them, and re-layouts  1.62 us
    pallas_call x1, Pallas kernels, gram_route(): pl.pallas_call(features_kernel, out_shape=jax.ShapeDtypeStruct((groups, m...  1.15 us

profile of v9, /device:TPU:0, one launch (start us, length us, event | category | flops | bytes accessed | tf_op | source)
XLA Modules:
  0.0 34.7 jit_solution(11397142075219802237)
XLA Ops:
  0.0 0.0 copy-start.2
  0.0 0.0 copy-start.1
  0.0 0.7 %copy-done.2 = s32[8]{0:T(128)S(1)} copy-done((s32[8]{0:T(128)S(1)}, s32[8]{0:T(128)}, u32[]{:S(2)}) %copy-start.2) | copy-done | bytes 56
  0.7 0.0 copy-done.1
  0.7 0.0 copy-start
  0.7 0.9 %copy-done = bf16[2,64,8,128]{3,2,1,0:T(8,128)(2,1)S(1)} copy-done((bf16[2,64,8,128]{3,2,1,0:T(8,128)(2,1)S(1)}, bf16[2,64,8,128]{3,2,1,0:T(8,128)(2,1)}, u32[]{:S(2)}) %copy-start) | copy-done | bytes 262168
  1.6 1.1 %shard_map.37 = bf16[4,8,64,128]{3,2,1,0:T(8,128)(2,1)S(1)} custom-call(s32[2]{0:T(128)S(1)} %copy-done.1, s32[8]{0:T(128)S(1)} %copy-done.2, bf16[2,512,128]{2,1,0:T(8,128)(2,1)S(1)} %bitcast.7), custom_call_target="tpu_custom_call" | custom-call | tf_op jit(solution)/shard_map/pallas_call | solution.py:277
  2.8 22.6 %all_to_all.5 = bf16[32,2,4096]{2,1,0:T(2,128)(2,1)S(1)} all-to-all(bf16[32,2,4096]{2,1,0:T(2,128)(2,1)S(1)} %bitcast.6), channel_id=1, replica_groups=mesh['grp'=4,'mod'=8] {'grp','mod'}, dimensions={0} | all-to-all | bytes 1048576 | tf_op jit(solution)/shard_map/all_to_all | solution.py:288
  25.4 0.2 reshape.15.leaf_ref
  25.6 9.0 %shard_map.38 = f32[1,16,4096]{2,1,0:T(8,128)} custom-call(bf16[64,4096]{1,0:T(8,128)(2,1)S(1)} %reshape.15.leaf_ref), custom_call_target="tpu_custom_call" | custom-call | tf_op jit(solution)/shard_map/pallas_call | solution.py:290
Async XLA Ops:
  0.0 0.7 %copy-start.2 = (s32[8]{0:T(128)S(1)}, s32[8]{0:T(128)}, u32[]{:S(2)}) copy-start(s32[8]{0:T(128)} %order_ref.1) | copy-start | bytes 100
  0.0 0.7 %copy-start.1 = (s32[2]{0:T(128)S(1)}, s32[2]{0:T(128)}, u32[]{:S(2)}) copy-start(s32[2]{0:T(128)} %lengths_ref.1) | copy-start | bytes 28
  0.7 0.9 %copy-start = (bf16[2,64,8,128]{3,2,1,0:T(8,128)(2,1)S(1)}, bf16[2,64,8,128]{3,2,1,0:T(8,128)(2,1)}, u32[]{:S(2)}) copy-start(bf16[2,64,8,128]{3,2,1,0:T(8,128)(2,1)} %param.3) | copy-start | bytes 786436

commit v10 on v9

--- a/solution.py
+++ b/solution.py
@@ -75,12 +75,35 @@
     return jax.vmap(precondition)(leaves, sketch)
 
 
+def terms(value):
+    first = value.astype(jnp.bfloat16)
+    left = value - first.astype(jnp.float32)
+    second = left.astype(jnp.bfloat16)
+    third = (left - second.astype(jnp.float32)).astype(jnp.bfloat16)
+    return first, second, third
+
+
+def small_dot(a, b, b_side):
+    rows = a.shape[0]
+    stacked = jnp.concatenate(terms(a), axis=0)
+    products = []
+    for k, term in enumerate(terms(b)):
+        products.append(
+            lax.dot_general(
+                stacked[: (3 - k) * rows], term, (((1,), (b_side,)), ((), ())), preferred_element_type=jnp.float32
+            )
+        )
+    large, middle, small = products
+    least = large[2 * rows :] + middle[rows:] + small
+    return large[:rows] + ((large[rows : 2 * rows] + middle[:rows]) + least)
+
+
 def dot_nt(a, b):
-    return lax.dot_general(a, b, (((1,), (1,)), ((), ())), precision=HI, preferred_element_type=jnp.float32)
+    return small_dot(a, b, 1)
 
 
 def dot_nn(a, b):
-    return jnp.dot(a, b, precision=HI, preferred_element_type=jnp.float32)
+    return small_dot(a, b, 0)
 
 
 def start_rows(count, width, span):

time: 34.8 us -> 34.6 us (level)
  no operation moved by 1% of the time
where the time goes in v10:
time: 34.6 us; the launch traced here: 34.4 us
  blocking collectives  22.6 us (65%)
  Pallas kernels  9.91 us (29%)
  local copies, waits for them, and re-layouts  1.82 us (5%)
    all_to_all x1, blocking collectives, gram_route(): lax.all_to_all(messages, ('grp', 'mod'), split_axis=0, concat_axis=0, til...  22.6 us
    pallas_call x1, Pallas kernels, gram_route(): pl.pallas_call(functools.partial(combine_kernel, rows), out_shape=jax.Sha...  8.76 us
    unnamed x6, local copies, waits for them, and re-layouts  1.62 us
    pallas_call x1, Pallas kernels, gram_route(): pl.pallas_call(features_kernel, out_shape=jax.ShapeDtypeStruct((groups, m...  1.15 us

profile of v10, /device:TPU:0, one launch (start us, length us, event | category | flops | bytes accessed | tf_op | source)
XLA Modules:
  0.0 34.4 jit_solution(6255032625404511355)
XLA Ops:
  0.0 0.0 copy-start.2
  0.0 0.0 copy-start.1
  0.0 0.7 %copy-done.2 = s32[8]{0:T(128)S(1)} copy-done((s32[8]{0:T(128)S(1)}, s32[8]{0:T(128)}, u32[]{:S(2)}) %copy-start.2) | copy-done | bytes 56
  0.7 0.0 copy-done.1
  0.7 0.0 copy-start
  0.7 0.9 %copy-done = bf16[2,64,8,128]{3,2,1,0:T(8,128)(2,1)S(1)} copy-done((bf16[2,64,8,128]{3,2,1,0:T(8,128)(2,1)S(1)}, bf16[2,64,8,128]{3,2,1,0:T(8,128)(2,1)}, u32[]{:S(2)}) %copy-start) | copy-done | bytes 262168
  1.6 1.2 %shard_map.37 = bf16[4,8,64,128]{3,2,1,0:T(8,128)(2,1)S(1)} custom-call(s32[2]{0:T(128)S(1)} %copy-done.1, s32[8]{0:T(128)S(1)} %copy-done.2, bf16[2,512,128]{2,1,0:T(8,128)(2,1)S(1)} %bitcast.7), custom_call_target="tpu_custom_call" | custom-call | tf_op jit(solution)/shard_map/pallas_call | solution.py:300
  2.8 22.6 %all_to_all.5 = bf16[32,2,4096]{2,1,0:T(2,128)(2,1)S(1)} all-to-all(bf16[32,2,4096]{2,1,0:T(2,128)(2,1)S(1)} %bitcast.6), channel_id=1, replica_groups=mesh['grp'=4,'mod'=8] {'grp','mod'}, dimensions={0} | all-to-all | bytes 1048576 | tf_op jit(solution)/shard_map/all_to_all | solution.py:311
  25.4 0.2 reshape.15.leaf_ref
  25.6 8.8 %shard_map.38 = f32[1,16,4096]{2,1,0:T(8,128)} custom-call(bf16[64,4096]{1,0:T(8,128)(2,1)S(1)} %reshape.15.leaf_ref), custom_call_target="tpu_custom_call" | custom-call | tf_op jit(solution)/shard_map/pallas_call | solution.py:313
Async XLA Ops:
  0.0 0.7 %copy-start.2 = (s32[8]{0:T(128)S(1)}, s32[8]{0:T(128)}, u32[]{:S(2)}) copy-start(s32[8]{0:T(128)} %order_ref.1) | copy-start | bytes 100
  0.0 0.7 %copy-start.1 = (s32[2]{0:T(128)S(1)}, s32[2]{0:T(128)}, u32[]{:S(2)}) copy-start(s32[2]{0:T(128)} %lengths_ref.1) | copy-start | bytes 28
  0.7 0.9 %copy-start = (bf16[2,64,8,128]{3,2,1,0:T(8,128)(2,1)S(1)}, bf16[2,64,8,128]{3,2,1,0:T(8,128)(2,1)}, u32[]{:S(2)}) copy-start(bf16[2,64,8,128]{3,2,1,0:T(8,128)(2,1)} %param.3) | copy-start | bytes 786436

commit v11 on v9

--- a/solution.py
+++ b/solution.py
@@ -111,6 +111,11 @@
     return columns
 
 
+def reciprocal(value):
+    guess = pl.reciprocal(value, approx=True)
+    return guess * (2.0 - value * guess)
+
+
 def eliminate(columns, rhs):
     count = len(columns)
     width = rhs.shape[1]
@@ -125,9 +130,9 @@
         b = left[home][at + 1 : at + 2]
         c = right[home][at + 1 : at + 2]
         det = a * c - b * b
-        ratio = b / a
+        ratio = b * reciprocal(a)
         diag[home] = jnp.where(row == at, a, jnp.where(row == at + 1, c - b * ratio, diag[home]))
-        inverse = 1.0 / det
+        inverse = reciprocal(det)
         ia, ib, ic = c * inverse, b * inverse, a * inverse
         low, high = {}, {}
         for k in left:
@@ -246,19 +251,19 @@
     lane = lax.broadcasted_iota(jnp.int32, (depth, full), 1)
     for e in range(examples):
         block = tokens_ref[e].astype(jnp.float32)
-        left = jnp.where(lane < half, block, 0.0).astype(jnp.bfloat16)
-        right = jnp.where(lane < half, 0.0, pltpu.roll(block, half, 1)).astype(jnp.bfloat16)
+        inputs = jnp.where(lane < half, block, 0.0).astype(jnp.bfloat16)
         grads = block.T[half:]
         for k in range(depth // full):
             grads_ref[k] = grads[:, k * full : (k + 1) * full]
         live = position < lengths_ref[e] * modules
-        flat = jnp.zeros((modules * chunks, full), jnp.float32)
-        for odd, side in ((0, left), (1, right)):
+        apiece = []
+        for odd in range(2):
             every = pl.ds(odd, chunks, stride=2)
             grads = jnp.concatenate([grads_ref[k, every, :] for k in range(depth // full)], axis=1)
             grads = jnp.where(live, grads, 0.0)
-            apiece = [jnp.where(module == q, grads, 0.0).astype(jnp.bfloat16) for q in range(modules)]
-            flat = flat + jnp.dot(jnp.concatenate(apiece, axis=0), side, preferred_element_type=jnp.float32)
+            apiece += [jnp.where(module == q, grads, 0.0).astype(jnp.bfloat16) for q in range(modules)]
+        both = jnp.dot(jnp.concatenate(apiece, axis=0), inputs, preferred_element_type=jnp.float32)
+        flat = both[: modules * chunks] + pltpu.roll(both[modules * chunks :], half, 1)
         held_ref[pl.ds(e, modules * chunks, stride=examples), :] = flat
     for slot in range(modules):
         first = pl.multiple_of(order_ref[slot] * pairs, pairs)

time: 34.8 us -> 35.2 us (1.011)
  no operation moved by 1% of the time
where the time goes in v11:
time: 35.2 us; the launch traced here: 35 us
  blocking collectives  22.7 us (64%)
  Pallas kernels  10.5 us (30%)
  local copies, waits for them, and re-layouts  1.82 us (5%)
    all_to_all x1, blocking collectives, gram_route(): lax.all_to_all(messages, ('grp', 'mod'), split_axis=0, concat_axis=0, til...  22.7 us
    pallas_call x1, Pallas kernels, gram_route(): pl.pallas_call(functools.partial(combine_kernel, rows), out_shape=jax.Sha...  9.33 us
    unnamed x6, local copies, waits for them, and re-layouts  1.62 us
    pallas_call x1, Pallas kernels, gram_route(): pl.pallas_call(features_kernel, out_shape=jax.ShapeDtypeStruct((groups, m...  1.16 us

profile of v11, /device:TPU:0, one launch (start us, length us, event | category | flops | bytes accessed | tf_op | source)
XLA Modules:
  0.0 35.0 jit_solution(4910559755697423371)
XLA Ops:
  0.0 0.0 copy-start.2
  0.0 0.0 copy-start.1
  0.0 0.7 %copy-done.2 = s32[8]{0:T(128)S(1)} copy-done((s32[8]{0:T(128)S(1)}, s32[8]{0:T(128)}, u32[]{:S(2)}) %copy-start.2) | copy-done | bytes 56
  0.7 0.0 copy-done.1
  0.7 0.0 copy-start
  0.7 0.9 %copy-done = bf16[2,64,8,128]{3,2,1,0:T(8,128)(2,1)S(1)} copy-done((bf16[2,64,8,128]{3,2,1,0:T(8,128)(2,1)S(1)}, bf16[2,64,8,128]{3,2,1,0:T(8,128)(2,1)}, u32[]{:S(2)}) %copy-start) | copy-done | bytes 262168
  1.6 1.2 %shard_map.37 = bf16[4,8,64,128]{3,2,1,0:T(8,128)(2,1)S(1)} custom-call(s32[2]{0:T(128)S(1)} %copy-done.1, s32[8]{0:T(128)S(1)} %copy-done.2, bf16[2,512,128]{2,1,0:T(8,128)(2,1)S(1)} %bitcast.7), custom_call_target="tpu_custom_call" | custom-call | tf_op jit(solution)/shard_map/pallas_call | solution.py:282
  2.8 22.7 %all_to_all.5 = bf16[32,2,4096]{2,1,0:T(2,128)(2,1)S(1)} all-to-all(bf16[32,2,4096]{2,1,0:T(2,128)(2,1)S(1)} %bitcast.6), channel_id=1, replica_groups=mesh['grp'=4,'mod'=8] {'grp','mod'}, dimensions={0} | all-to-all | bytes 1048576 | tf_op jit(solution)/shard_map/all_to_all | solution.py:293
  25.4 0.2 reshape.15.leaf_ref
  25.6 9.3 %shard_map.38 = f32[1,16,4096]{2,1,0:T(8,128)} custom-call(bf16[64,4096]{1,0:T(8,128)(2,1)S(1)} %reshape.15.leaf_ref), custom_call_target="tpu_custom_call" | custom-call | tf_op jit(solution)/shard_map/pallas_call | solution.py:295
Async XLA Ops:
  0.0 0.7 %copy-start.2 = (s32[8]{0:T(128)S(1)}, s32[8]{0:T(128)}, u32[]{:S(2)}) copy-start(s32[8]{0:T(128)} %order_ref.1) | copy-start | bytes 100
  0.0 0.7 %copy-start.1 = (s32[2]{0:T(128)S(1)}, s32[2]{0:T(128)}, u32[]{:S(2)}) copy-start(s32[2]{0:T(128)} %lengths_ref.1) | copy-start | bytes 28
  0.7 0.9 %copy-start = (bf16[2,64,8,128]{3,2,1,0:T(8,128)(2,1)S(1)}, bf16[2,64,8,128]{3,2,1,0:T(8,128)(2,1)}, u32[]{:S(2)}) copy-start(bf16[2,64,8,128]{3,2,1,0:T(8,128)(2,1)} %param.3) | copy-start | bytes 786436

commit v12 on v9

--- a/solution.py
+++ b/solution.py
@@ -212,9 +212,7 @@
     return solved[:, :count], solved[:, count:], enough
 
 
-def combine_kernel(rows, leaf_ref, out_ref, gram_ref, change_ref):
-    leaf = leaf_ref[...]
-    gram_ref[...] = lax.dot_general(leaf, leaf, (((1,), (1,)), ((), ())), preferred_element_type=jnp.float32)
+def combine_kernel(rows, gram_ref, leaf_ref, out_ref, change_ref):
     own = pl.ds(pl.multiple_of(lax.axis_index("grp") * rows, rows), rows)
 
     def finish(often):
@@ -287,12 +285,13 @@
     messages = messages.reshape(groups * modules, chunks, own, full).transpose(0, 2, 1, 3).reshape(groups * modules, own, width)
     leaf = lax.all_to_all(messages, ("grp", "mod"), split_axis=0, concat_axis=0, tiled=True)
     leaf = leaf.reshape(count, width)
+    gram = lax.dot_general(leaf, leaf, (((1,), (1,)), ((), ())), preferred_element_type=jnp.float32)
     return pl.pallas_call(
         functools.partial(combine_kernel, rows),
         out_shape=jax.ShapeDtypeStruct((1, rows, width), jnp.float32),
-        scratch_shapes=[pltpu.VMEM((count, count), jnp.float32)] * 2,
+        scratch_shapes=[pltpu.VMEM((count, count), jnp.float32)],
         compiler_params=pltpu.CompilerParams(vmem_limit_bytes=VMEM_BYTES),
-    )(leaf)
+    )(gram, leaf)
 
 
 def local_features(token_block, live_counts):

time: 34.8 us -> 34.8 us (level)
  no operation moved by 1% of the time
where the time goes in v12:
time: 34.8 us; the launch traced here: 34.6 us
  blocking collectives  22.6 us (65%)
  Pallas kernels  9.87 us (28%)
  local copies, waits for them, and re-layouts  1.82 us (5%)
    all_to_all x1, blocking collectives, gram_route(): lax.all_to_all(messages, ('grp', 'mod'), split_axis=0, concat_axis=0, til...  22.6 us
    pallas_call x1, Pallas kernels, gram_route(): pl.pallas_call(functools.partial(combine_kernel, rows), out_shape=jax.Sha...  8.72 us
    unnamed x6, local copies, waits for them, and re-layouts  1.62 us
    pallas_call x1, Pallas kernels, gram_route(): pl.pallas_call(features_kernel, out_shape=jax.ShapeDtypeStruct((groups, m...  1.15 us

profile of v12, /device:TPU:0, one launch (start us, length us, event | category | flops | bytes accessed | tf_op | source)
XLA Modules:
  0.0 34.6 jit_solution(1513766411180196229)
XLA Ops:
  0.0 0.0 copy-start.2
  0.0 0.0 copy-start.1
  0.0 0.7 %copy-done.2 = s32[8]{0:T(128)S(1)} copy-done((s32[8]{0:T(128)S(1)}, s32[8]{0:T(128)}, u32[]{:S(2)}) %copy-start.2) | copy-done | bytes 56
  0.7 0.0 copy-done.1
  0.7 0.0 copy-start
  0.7 0.9 %copy-done = bf16[2,64,8,128]{3,2,1,0:T(8,128)(2,1)S(1)} copy-done((bf16[2,64,8,128]{3,2,1,0:T(8,128)(2,1)S(1)}, bf16[2,64,8,128]{3,2,1,0:T(8,128)(2,1)}, u32[]{:S(2)}) %copy-start) | copy-done | bytes 262168
  1.6 1.1 %shard_map.37 = bf16[4,8,64,128]{3,2,1,0:T(8,128)(2,1)S(1)} custom-call(s32[2]{0:T(128)S(1)} %copy-done.1, s32[8]{0:T(128)S(1)} %copy-done.2, bf16[2,512,128]{2,1,0:T(8,128)(2,1)S(1)} %bitcast.9), custom_call_target="tpu_custom_call" | custom-call | tf_op jit(solution)/shard_map/pallas_call | solution.py:275
  2.8 22.6 %all_to_all.5 = bf16[32,2,4096]{2,1,0:T(2,128)(2,1)S(1)} all-to-all(bf16[32,2,4096]{2,1,0:T(2,128)(2,1)S(1)} %bitcast.8), channel_id=1, replica_groups=mesh['grp'=4,'mod'=8] {'grp','mod'}, dimensions={0} | all-to-all | bytes 1048576 | tf_op jit(solution)/shard_map/all_to_all | solution.py:286
  25.4 0.2 reshape.15.leaf_ref
  25.6 0.3 fusion.gram_ref
  25.9 8.7 %shard_map.38 = f32[1,16,4096]{2,1,0:T(8,128)} custom-call(f32[64,64]{1,0:T(8,128)S(1)} %fusion.gram_ref, bf16[64,4096]{1,0:T(8,128)(2,1)S(1)} %reshape.15.leaf_ref), custom_call_target="tpu_custom_call" | custom-call | tf_op jit(solution)/shard_map/pallas_call | solution.py:289
Async XLA Ops:
  0.0 0.7 %copy-start.2 = (s32[8]{0:T(128)S(1)}, s32[8]{0:T(128)}, u32[]{:S(2)}) copy-start(s32[8]{0:T(128)} %order_ref.1) | copy-start | bytes 100
  0.0 0.7 %copy-start.1 = (s32[2]{0:T(128)S(1)}, s32[2]{0:T(128)}, u32[]{:S(2)}) copy-start(s32[2]{0:T(128)} %lengths_ref.1) | copy-start | bytes 28
  0.7 0.9 %copy-start = (bf16[2,64,8,128]{3,2,1,0:T(8,128)(2,1)S(1)}, bf16[2,64,8,128]{3,2,1,0:T(8,128)(2,1)}, u32[]{:S(2)}) copy-start(bf16[2,64,8,128]{3,2,1,0:T(8,128)(2,1)} %param.3) | copy-start | bytes 786436

commit v13 on v9

--- a/solution.py
+++ b/solution.py
@@ -12,6 +12,7 @@
 ITERS = 3
 HI = lax.Precision.HIGHEST
 VMEM_BYTES = 48 * 1024 * 1024
+FETCH_BYTES = 56 * 1024 * 1024
 
 
 def partner(value, axis, bit):
@@ -236,15 +237,27 @@
         finish(True)
 
 
-def features_kernel(lengths_ref, order_ref, tokens_ref, out_ref, grads_ref, held_ref):
+def features_kernel(
+    lengths_hbm, order_hbm, tokens_hbm, out_hbm, lengths_ref, order_ref, tokens_ref, grads_ref, held_ref, out_ref, sems
+):
     examples, depth, full = tokens_ref.shape
-    groups, modules, pairs, _ = out_ref.shape
+    groups, modules, pairs, _ = out_hbm.shape
     half = full // 2
     chunks = pairs // examples
+    small = [
+        pltpu.make_async_copy(lengths_hbm, lengths_ref, sems.at[0]),
+        pltpu.make_async_copy(order_hbm, order_ref, sems.at[1]),
+    ]
+    large = [pltpu.make_async_copy(tokens_hbm.at[e], tokens_ref.at[e], sems.at[2 + e]) for e in range(examples)]
+    for copy in small + large:
+        copy.start()
     position = lax.broadcasted_iota(jnp.int32, (chunks, depth), 1)
     module = lax.rem(position, modules)
     lane = lax.broadcasted_iota(jnp.int32, (depth, full), 1)
+    for copy in small:
+        copy.wait()
     for e in range(examples):
+        large[e].wait()
         block = tokens_ref[e].astype(jnp.float32)
         left = jnp.where(lane < half, block, 0.0).astype(jnp.bfloat16)
         right = jnp.where(lane < half, 0.0, pltpu.roll(block, half, 1)).astype(jnp.bfloat16)
@@ -260,11 +273,16 @@
             apiece = [jnp.where(module == q, grads, 0.0).astype(jnp.bfloat16) for q in range(modules)]
             flat = flat + jnp.dot(jnp.concatenate(apiece, axis=0), side, preferred_element_type=jnp.float32)
         held_ref[pl.ds(e, modules * chunks, stride=examples), :] = flat
+    sent = []
     for slot in range(modules):
         first = pl.multiple_of(order_ref[slot] * pairs, pairs)
-        message = held_ref[pl.ds(first, pairs), :].astype(jnp.bfloat16)
+        out_ref[slot] = held_ref[pl.ds(first, pairs), :].astype(jnp.bfloat16)
         for g in range(groups):
-            out_ref[g, slot] = message
+            at = 2 + examples + slot * groups + g
+            sent.append(pltpu.make_async_copy(out_ref.at[slot], out_hbm.at[g, slot], sems.at[at]))
+            sent[-1].start()
+    for copy in sent:
+        copy.wait()
 
 
 def gram_route(tokens, lengths, module_order):
@@ -277,12 +295,18 @@
     messages = pl.pallas_call(
         features_kernel,
         out_shape=jax.ShapeDtypeStruct((groups, modules, chunks * own, full), jnp.bfloat16),
-        in_specs=[pl.BlockSpec(memory_space=space) for space in (pltpu.SMEM, pltpu.SMEM, pltpu.VMEM)],
+        in_specs=[pl.BlockSpec(memory_space=pl.ANY)] * 3,
+        out_specs=pl.BlockSpec(memory_space=pl.ANY),
         scratch_shapes=[
+            pltpu.SMEM(lengths.shape, jnp.int32),
+            pltpu.SMEM(module_order.shape, jnp.int32),
+            pltpu.VMEM((own, slots * modules, full), jnp.bfloat16),
             pltpu.VMEM((slots * modules // full, full // 2, full), jnp.float32),
             pltpu.VMEM((modules * chunks * own, full), jnp.float32),
+            pltpu.VMEM((modules, chunks * own, full), jnp.bfloat16),
+            pltpu.SemaphoreType.DMA((2 + own + modules * groups,)),
         ],
-        compiler_params=pltpu.CompilerParams(vmem_limit_bytes=VMEM_BYTES),
+        compiler_params=pltpu.CompilerParams(vmem_limit_bytes=FETCH_BYTES),
     )(lengths, module_order, tokens.reshape(own, slots * modules, full))
     messages = messages.reshape(groups * modules, chunks, own, full).transpose(0, 2, 1, 3).reshape(groups * modules, own, width)
     leaf = lax.all_to_all(messages, ("grp", "mod"), split_axis=0, concat_axis=0, tiled=True)

time: 34.8 us -> 35.2 us (1.011)
  Pallas kernels: 10.2 us -> 11.9 us
  local copies, waits for them, and re-layouts: 1.82 us -> 0.2 us
    pallas_call x1, Pallas kernels: 1.15 us -> 2.88 us  [gram_route(): pl.pallas_call(features_kernel, out_shape=jax.ShapeDtypeStruct((groups, m...]
    unnamed x6 -> x0, local copies, waits for them, and re-layouts: 1.62 us -> none
where the time goes in v13:
time: 35.2 us; the launch traced here: 35 us
  blocking collectives  22.9 us (65%)
  Pallas kernels  11.9 us (34%)
    all_to_all x1, blocking collectives, gram_route(): lax.all_to_all(messages, ('grp', 'mod'), split_axis=0, concat_axis=0, til...  22.9 us
    pallas_call x1, Pallas kernels, gram_route(): pl.pallas_call(functools.partial(combine_kernel, rows), out_shape=jax.Sha...  9.02 us
    pallas_call x1, Pallas kernels, gram_route(): pl.pallas_call(features_kernel, out_shape=jax.ShapeDtypeStruct((groups, m...  2.88 us

profile of v13, /device:TPU:0, one launch (start us, length us, event | category | flops | bytes accessed | tf_op | source)
XLA Modules:
  0.0 35.0 jit_solution(12763126147507906295)
XLA Ops:
  0.0 2.9 %shard_map.37 = bf16[4,8,64,128]{3,2,1,0:T(8,128)(2,1)} custom-call(s32[2]{0:T(128)} %lengths_hbm.1, s32[8]{0:T(128)} %order_hbm.1, bf16[2,512,128]{2,1,0:T(8,128)(2,1)} %bitcast.7), custom_call_target="tpu_custom_call" | custom-call | tf_op jit(solution)/shard_map/pallas_call | solution.py:295
  2.9 22.9 %all_to_all.5 = bf16[32,2,4096]{2,1,0:T(2,128)(2,1)S(1)} all-to-all(bf16[32,2,4096]{2,1,0:T(2,128)(2,1)} %bitcast.6), channel_id=1, replica_groups=mesh['grp'=4,'mod'=8] {'grp','mod'}, dimensions={0} | all-to-all | bytes 1048576 | tf_op jit(solution)/shard_map/all_to_all | solution.py:312
  25.8 0.2 reshape.15.leaf_ref
  26.0 9.0 %shard_map.38 = f32[1,16,4096]{2,1,0:T(8,128)} custom-call(bf16[64,4096]{1,0:T(8,128)(2,1)S(1)} %reshape.15.leaf_ref), custom_call_target="tpu_custom_call" | custom-call | tf_op jit(solution)/shard_map/pallas_call | solution.py:314

commit v14 on v9

--- a/solution.py
+++ b/solution.py
@@ -238,7 +238,7 @@
 
 def features_kernel(lengths_ref, order_ref, tokens_ref, out_ref, grads_ref, held_ref):
     examples, depth, full = tokens_ref.shape
-    groups, modules, pairs, _ = out_ref.shape
+    modules, groups, pairs, _ = out_ref.shape
     half = full // 2
     chunks = pairs // examples
     position = lax.broadcasted_iota(jnp.int32, (chunks, depth), 1)
@@ -264,7 +264,7 @@
         first = pl.multiple_of(order_ref[slot] * pairs, pairs)
         message = held_ref[pl.ds(first, pairs), :].astype(jnp.bfloat16)
         for g in range(groups):
-            out_ref[g, slot] = message
+            out_ref[slot, g] = message
 
 
 def gram_route(tokens, lengths, module_order):
@@ -276,7 +276,7 @@
     chunks = width // full
     messages = pl.pallas_call(
         features_kernel,
-        out_shape=jax.ShapeDtypeStruct((groups, modules, chunks * own, full), jnp.bfloat16),
+        out_shape=jax.ShapeDtypeStruct((modules, groups, chunks * own, full), jnp.bfloat16),
         in_specs=[pl.BlockSpec(memory_space=space) for space in (pltpu.SMEM, pltpu.SMEM, pltpu.VMEM)],
         scratch_shapes=[
             pltpu.VMEM((slots * modules // full, full // 2, full), jnp.float32),
@@ -285,8 +285,8 @@
         compiler_params=pltpu.CompilerParams(vmem_limit_bytes=VMEM_BYTES),
     )(lengths, module_order, tokens.reshape(own, slots * modules, full))
     messages = messages.reshape(groups * modules, chunks, own, full).transpose(0, 2, 1, 3).reshape(groups * modules, own, width)
-    leaf = lax.all_to_all(messages, ("grp", "mod"), split_axis=0, concat_axis=0, tiled=True)
-    leaf = leaf.reshape(count, width)
+    leaf = lax.all_to_all(messages, ("mod", "grp"), split_axis=0, concat_axis=0, tiled=True)
+    leaf = leaf.reshape(modules, groups, own, width).transpose(1, 0, 2, 3).reshape(count, width)
     return pl.pallas_call(
         functools.partial(combine_kernel, rows),
         out_shape=jax.ShapeDtypeStruct((1, rows, width), jnp.float32),

time: 34.8 us -> 34.9 us (level)
  the two profiles are of different devices: /device:TPU:0 before, /device:TPU:1 now
where the time goes in v14:
time: 34.9 us; the launch traced here: 34.7 us
  blocking collectives  22.2 us (64%)
  Pallas kernels  10.2 us (29%)
  local copies, waits for them, and re-layouts  2.28 us (7%)
    all_to_all x1, blocking collectives, gram_route(): lax.all_to_all(messages, ('mod', 'grp'), split_axis=0, concat_axis=0, til...  22.2 us
    pallas_call x1, Pallas kernels, gram_route(): pl.pallas_call(functools.partial(combine_kernel, rows), out_shape=jax.Sha...  9.02 us
    unnamed x6, local copies, waits for them, and re-layouts  1.62 us
    pallas_call x1, Pallas kernels, gram_route(): pl.pallas_call(features_kernel, out_shape=jax.ShapeDtypeStruct((modules,...  1.15 us

profile of v14, /device:TPU:1, one launch (start us, length us, event | category | flops | bytes accessed | tf_op | source)
XLA Modules:
  0.0 34.7 jit_solution(17792250396844076959)
XLA Ops:
  0.0 0.0 copy-start.2
  0.0 0.0 copy-start.1
  0.0 0.7 %copy-done.2 = s32[8]{0:T(128)S(1)} copy-done((s32[8]{0:T(128)S(1)}, s32[8]{0:T(128)}, u32[]{:S(2)}) %copy-start.2) | copy-done | bytes 56
  0.7 0.0 copy-done.1
  0.7 0.0 copy-start
  0.7 0.9 %copy-done = bf16[2,64,8,128]{3,2,1,0:T(8,128)(2,1)S(1)} copy-done((bf16[2,64,8,128]{3,2,1,0:T(8,128)(2,1)S(1)}, bf16[2,64,8,128]{3,2,1,0:T(8,128)(2,1)}, u32[]{:S(2)}) %copy-start) | copy-done | bytes 262168
  1.6 1.1 %shard_map.37 = bf16[8,4,64,128]{3,2,1,0:T(8,128)(2,1)S(1)} custom-call(s32[2]{0:T(128)S(1)} %copy-done.1, s32[8]{0:T(128)S(1)} %copy-done.2, bf16[2,512,128]{2,1,0:T(8,128)(2,1)S(1)} %bitcast.10), custom_call_target="tpu_custom_call" | custom-call | tf_op jit(solution)/shard_map/pallas_call | solution.py:277
  2.8 22.2 %all_to_all.5 = bf16[32,2,4096]{2,1,0:T(2,128)(2,1)S(1)} all-to-all(bf16[32,2,4096]{2,1,0:T(2,128)(2,1)S(1)} %bitcast.9), channel_id=1, replica_groups=mesh['grp'=4,'mod'=8] {'mod','grp'}, dimensions={0} | all-to-all | bytes 1048576 | tf_op jit(solution)/shard_map/all_to_all | solution.py:288
  25.0 0.5 %copy.4 = bf16[4,8,2,4096]{3,2,1,0:T(2,128)(2,1)S(1)} copy(bf16[4,8,2,4096]{3,2,0,1:T(2,128)(2,1)S(1)} %bitcast.11) | data formatting | bytes 1048576 | tf_op jit(solution)/shard_map/transpose | solution.py:289
  25.4 0.2 reshape.19.leaf_ref
  25.7 9.0 %shard_map.38 = f32[1,16,4096]{2,1,0:T(8,128)} custom-call(bf16[64,4096]{1,0:T(8,128)(2,1)S(1)} %reshape.19.leaf_ref), custom_call_target="tpu_custom_call" | custom-call | tf_op jit(solution)/shard_map/pallas_call | solution.py:290
Async XLA Ops:
  0.0 0.7 %copy-start.2 = (s32[8]{0:T(128)S(1)}, s32[8]{0:T(128)}, u32[]{:S(2)}) copy-start(s32[8]{0:T(128)} %order_ref.1) | copy-start | bytes 100
  0.0 0.7 %copy-start.1 = (s32[2]{0:T(128)S(1)}, s32[2]{0:T(128)}, u32[]{:S(2)}) copy-start(s32[2]{0:T(128)} %lengths_ref.1) | copy-start | bytes 28
  0.7 0.9 %copy-start = (bf16[2,64,8,128]{3,2,1,0:T(8,128)(2,1)S(1)}, bf16[2,64,8,128]{3,2,1,0:T(8,128)(2,1)}, u32[]{:S(2)}) copy-start(bf16[2,64,8,128]{3,2,1,0:T(8,128)(2,1)} %param.3) | copy-start | bytes 786436

commit v15 on v14

--- a/solution.py
+++ b/solution.py
@@ -83,10 +83,9 @@
     return jnp.dot(a, b, precision=HI, preferred_element_type=jnp.float32)
 
 
-def start_rows(count, width, span):
-    j = lax.broadcasted_iota(jnp.int32, (count, width), 0)
-    i = lax.rem(lax.broadcasted_iota(jnp.int32, (count, width), 1), span)
-    turn = lax.rem((2 * i + 1) * (2 * j + 1), 8 * span)
+def start_rows(count, index, span):
+    j = lax.broadcasted_iota(jnp.int32, (count, index.shape[1]), 0)
+    turn = lax.rem((2 * index + 1) * (2 * j + 1), 8 * span)
     folded = jnp.minimum(turn, 8 * span - turn)
     angle = (2 * span - folded).astype(jnp.float32) * (math.pi / (4 * span))
     square = angle * angle
@@ -96,8 +95,8 @@
     return angle * series
 
 
-def spread(gram, problems, count, width):
-    lane = lax.broadcasted_iota(jnp.int32, (8, width), 1)
+def spread(gram, count, width, near=None):
+    problems = 1 if near is None else 2
     columns = []
     for j in range(count):
         blocks = {}
@@ -106,7 +105,7 @@
                 jnp.broadcast_to(gram[8 * b : 8 * b + 8, k * count + j : k * count + j + 1], (8, width))
                 for k in range(problems)
             ]
-            blocks[b] = parts[0] if problems == 1 else jnp.where(lane < width // 2, parts[0], parts[1])
+            blocks[b] = parts[0] if near is None else jnp.where(near, parts[0], parts[1])
         columns.append(blocks)
     return columns
 
@@ -146,59 +145,65 @@
     return jnp.concatenate([part * lax.rsqrt(d) for part, d in zip(parts, diag)], axis=0), worst
 
 
-def apart(value):
-    lane = lax.broadcasted_iota(jnp.int32, value.shape, 1)
-    near = lane < value.shape[1] // 2
+def apart(value, near):
     return jnp.concatenate([jnp.where(near, value, 0.0), jnp.where(near, 0.0, value)], axis=0)
 
 
-def solve_small(gram, rows, often):
+def place(position, groups, own, rows):
+    group = lax.rem(lax.div(position, own), groups)
+    example = lax.div(position, own * groups) * own + lax.rem(position, own)
+    return group < groups // 2, lax.rem(group, groups // 2) * rows + example
+
+
+def solve_small(gram, rows, groups, own, often):
     count = gram.shape[0]
     half = count // 2
     r = lax.broadcasted_iota(jnp.int32, gram.shape, 0)
     c = lax.broadcasted_iota(jnp.int32, gram.shape, 1)
-    lane = lax.broadcasted_iota(jnp.int32, (1, count), 1)
+    near_row, _ = place(r, groups, own, rows)
+    near_col, index = place(c, groups, own, rows)
+    near, index = near_col[:rows], index[:rows]
     diagonal = jnp.sum(jnp.where(r == c, gram, 0.0), axis=0, keepdims=True)
-    trace_lower = jnp.sum(jnp.where(lane < half, diagonal, 0.0), axis=1, keepdims=True)
-    trace_upper = jnp.sum(jnp.where(lane < half, 0.0, diagonal), axis=1, keepdims=True)
+    trace_lower = jnp.sum(jnp.where(near[:1], diagonal, 0.0), axis=1, keepdims=True)
+    trace_upper = jnp.sum(jnp.where(near[:1], 0.0, diagonal), axis=1, keepdims=True)
     scale = 1.0 / (trace_lower + trace_upper)
-    pair_scale = 1.0 / jnp.where(lane < half, trace_lower, trace_upper)
-    own_pair = jnp.where((r < half) == (c < half), gram, 0.0)
-
-    moved = dot_nn(start_rows(rows, count, half), own_pair) * pair_scale
+    pair_scale = 1.0 / jnp.where(near[:1], trace_lower, trace_upper)
+    own_pair = jnp.where(jnp.logical_xor(near_row, near_col), 0.0, gram)
+
+    moved = dot_nn(start_rows(rows, index, half), own_pair) * pair_scale
     own_pair = own_pair * pair_scale
     smallest = []
     if not often:
         moved = dot_nn(moved, own_pair)
     for onward_too in (True, True, False, False) if often else (True, False):
-        inner = dot_nt(moved, apart(moved))
+        inner = dot_nt(moved, apart(moved, near))
         onward = dot_nn(moved, own_pair) if onward_too else moved
-        moved, worst = eliminate(spread(inner, 2, rows, count), onward)
+        moved, worst = eliminate(spread(inner, rows, count, near[:8]), onward)
         smallest.append(jnp.min(worst))
-    basis = apart(moved)
+    basis = apart(moved, near)
 
     gram = gram * scale
     reached = dot_nn(basis, gram)
     kernel = dot_nt(reached, basis)
-    moved = dot_nn(start_rows(rows, half, half), kernel)
+    moved = dot_nn(start_rows(rows, c[:rows, :half], half), kernel)
     if often:
         for onward_too in (True, True, False):
             inner = dot_nt(moved, moved)
             onward = dot_nn(moved, kernel) if onward_too else moved
-            moved, _ = eliminate(spread(inner, 1, rows, half), onward)
+            moved, _ = eliminate(spread(inner, rows, half), onward)
     else:
         moved = dot_nn(moved, dot_nn(kernel, kernel))
     inner = dot_nt(moved, moved)
     onward = dot_nn(moved, jnp.concatenate([reached, basis], axis=1))
-    both, worst = eliminate(spread(inner, 1, rows, 2 * count), onward)
+    both, worst = eliminate(spread(inner, rows, 2 * count), onward)
     smallest.append(jnp.min(worst))
     enough = jnp.logical_and(jnp.logical_and(smallest[0] > 1e-4, smallest[1] > 1e-2), smallest[-1] > 3e-4)
 
     weights = both[:, count:]
     row = lax.broadcasted_iota(jnp.int32, (8, 2 * count), 0)
     joint = dot_nt(jnp.concatenate([both[:, :count], weights], axis=0), weights)
-    energy = spread(joint[:rows], 1, rows, 2 * count)
-    metric = spread(joint[rows:], 1, rows, 2 * count)
+    energy = spread(joint[:rows], rows, 2 * count)
+    metric = spread(joint[rows:], rows, 2 * count)
     total = jnp.zeros((8, 2 * count), jnp.float32)
     for j in range(rows):
         for b in energy[j]:
@@ -212,21 +217,28 @@
     return solved[:, :count], solved[:, count:], enough
 
 
-def combine_kernel(rows, leaf_ref, out_ref, gram_ref, change_ref):
+def combine_kernel(rows, groups, own, leaf_ref, out_ref, gram_ref, change_ref, mine_ref):
     leaf = leaf_ref[...]
+    count = leaf.shape[0]
     gram_ref[...] = lax.dot_general(leaf, leaf, (((1,), (1,)), ((), ())), preferred_element_type=jnp.float32)
-    own = pl.ds(pl.multiple_of(lax.axis_index("grp") * rows, rows), rows)
+    group = lax.axis_index("grp")
+    row = lax.broadcasted_iota(jnp.int32, (rows, count), 0)
+    lane = lax.broadcasted_iota(jnp.int32, (rows, count), 1)
+    chosen = lane == lax.div(row, own) * (own * groups) + group * own + lax.rem(row, own)
 
     def finish(often):
-        projected, weights, enough = solve_small(gram_ref[...], rows, often)
-        change_ref[...] = lax.dot_general(
+        projected, weights, enough = solve_small(gram_ref[...], rows, groups, own, often)
+        change_ref[:, :count] = lax.dot_general(
             projected, weights, (((0,), (0,)), ((), ())), precision=HI, preferred_element_type=jnp.float32
         )
-        change = change_ref[own, :]
-        top = change.astype(jnp.bfloat16)
-        rest = (change - top.astype(jnp.float32)).astype(jnp.bfloat16)
+        owners = rows // own
+        for e in range(own):
+            mine_ref[pl.ds(e, owners, stride=own), :] = change_ref[pl.ds(group * own + e, owners, stride=own * groups), :]
+        kept = jnp.where(chosen, 1.0, 0.0) - mine_ref[:, :count]
+        top = kept.astype(jnp.bfloat16)
+        rest = (kept - top.astype(jnp.float32)).astype(jnp.bfloat16)
         moved = jnp.dot(jnp.concatenate([top, rest], axis=0), leaf_ref[...], preferred_element_type=jnp.float32)
-        out_ref[0] = leaf_ref[own, :].astype(jnp.float32) - (moved[:rows] + moved[rows:])
+        out_ref[0] = moved[:rows] + moved[rows:]
         return enough
 
     enough = finish(False)
@@ -286,11 +298,11 @@
     )(lengths, module_order, tokens.reshape(own, slots * modules, full))
     messages = messages.reshape(groups * modules, chunks, own, full).transpose(0, 2, 1, 3).reshape(groups * modules, own, width)
     leaf = lax.all_to_all(messages, ("mod", "grp"), split_axis=0, concat_axis=0, tiled=True)
-    leaf = leaf.reshape(modules, groups, own, width).transpose(1, 0, 2, 3).reshape(count, width)
+    leaf = leaf.reshape(count, width)
     return pl.pallas_call(
-        functools.partial(combine_kernel, rows),
+        functools.partial(combine_kernel, rows, groups, own),
         out_shape=jax.ShapeDtypeStruct((1, rows, width), jnp.float32),
-        scratch_shapes=[pltpu.VMEM((count, count), jnp.float32)] * 2,
+        scratch_shapes=[pltpu.VMEM(shape, jnp.float32) for shape in ((count, count), (count, full), (rows, full))],
         compiler_params=pltpu.CompilerParams(vmem_limit_bytes=VMEM_BYTES),
     )(leaf)
 

time: 34.9 us -> 34.4 us (0.986)
  local copies, waits for them, and re-layouts: 2.28 us -> 1.82 us
    transpose x1 -> x0, local copies, waits for them, and re-layouts: 0.46 us -> none  [gram_route(): leaf.reshape(modules, groups, own, width).transpose(1, 0, 2, 3)]
where the time goes in v15:
time: 34.4 us; the launch traced here: 34.2 us
  blocking collectives  22.2 us (65%)
  Pallas kernels  10.2 us (30%)
  local copies, waits for them, and re-layouts  1.82 us (5%)
    all_to_all x1, blocking collectives, gram_route(): lax.all_to_all(messages, ('mod', 'grp'), split_axis=0, concat_axis=0, til...  22.2 us
    pallas_call x1, Pallas kernels, gram_route(): pl.pallas_call(functools.partial(combine_kernel, rows, groups, own), out_...  9.05 us
    unnamed x6, local copies, waits for them, and re-layouts  1.62 us
    pallas_call x1, Pallas kernels, gram_route(): pl.pallas_call(features_kernel, out_shape=jax.ShapeDtypeStruct((modules,...  1.15 us

profile of v15, /device:TPU:1, one launch (start us, length us, event | category | flops | bytes accessed | tf_op | source)
XLA Modules:
  0.0 34.2 jit_solution(10893636940498424159)
XLA Ops:
  0.0 0.0 copy-start.2
  0.0 0.0 copy-start.1
  0.0 0.7 %copy-done.2 = s32[8]{0:T(128)S(1)} copy-done((s32[8]{0:T(128)S(1)}, s32[8]{0:T(128)}, u32[]{:S(2)}) %copy-start.2) | copy-done | bytes 56
  0.7 0.0 copy-done.1
  0.7 0.0 copy-start
  0.7 0.9 %copy-done = bf16[2,64,8,128]{3,2,1,0:T(8,128)(2,1)S(1)} copy-done((bf16[2,64,8,128]{3,2,1,0:T(8,128)(2,1)S(1)}, bf16[2,64,8,128]{3,2,1,0:T(8,128)(2,1)}, u32[]{:S(2)}) %copy-start) | copy-done | bytes 262168
  1.6 1.1 %shard_map.37 = bf16[8,4,64,128]{3,2,1,0:T(8,128)(2,1)S(1)} custom-call(s32[2]{0:T(128)S(1)} %copy-done.1, s32[8]{0:T(128)S(1)} %copy-done.2, bf16[2,512,128]{2,1,0:T(8,128)(2,1)S(1)} %bitcast.7), custom_call_target="tpu_custom_call" | custom-call | tf_op jit(solution)/shard_map/pallas_call | solution.py:289
  2.8 22.2 %all_to_all.5 = bf16[32,2,4096]{2,1,0:T(2,128)(2,1)S(1)} all-to-all(bf16[32,2,4096]{2,1,0:T(2,128)(2,1)S(1)} %bitcast.6), channel_id=1, replica_groups=mesh['grp'=4,'mod'=8] {'mod','grp'}, dimensions={0} | all-to-all | bytes 1048576 | tf_op jit(solution)/shard_map/all_to_all | solution.py:300
  25.0 0.2 reshape.15.leaf_ref
  25.2 9.1 %shard_map.38 = f32[1,16,4096]{2,1,0:T(8,128)} custom-call(bf16[64,4096]{1,0:T(8,128)(2,1)S(1)} %reshape.15.leaf_ref), custom_call_target="tpu_custom_call" | custom-call | tf_op jit(solution)/shard_map/pallas_call | solution.py:302
Async XLA Ops:
  0.0 0.7 %copy-start.2 = (s32[8]{0:T(128)S(1)}, s32[8]{0:T(128)}, u32[]{:S(2)}) copy-start(s32[8]{0:T(128)} %order_ref.1) | copy-start | bytes 100
  0.0 0.7 %copy-start.1 = (s32[2]{0:T(128)S(1)}, s32[2]{0:T(128)}, u32[]{:S(2)}) copy-start(s32[2]{0:T(128)} %lengths_ref.1) | copy-start | bytes 28
  0.7 0.9 %copy-start = (bf16[2,64,8,128]{3,2,1,0:T(8,128)(2,1)S(1)}, bf16[2,64,8,128]{3,2,1,0:T(8,128)(2,1)}, u32[]{:S(2)}) copy-start(bf16[2,64,8,128]{3,2,1,0:T(8,128)(2,1)} %param.3) | copy-start | bytes 786436

commit v16 on v15

--- a/solution.py
+++ b/solution.py
@@ -200,19 +200,12 @@
     enough = jnp.logical_and(jnp.logical_and(smallest[0] > 1e-4, smallest[1] > 1e-2), smallest[-1] > 3e-4)
 
     weights = both[:, count:]
-    row = lax.broadcasted_iota(jnp.int32, (8, 2 * count), 0)
     joint = dot_nt(jnp.concatenate([both[:, :count], weights], axis=0), weights)
-    energy = spread(joint[:rows], rows, 2 * count)
-    metric = spread(joint[rows:], rows, 2 * count)
-    total = jnp.zeros((8, 2 * count), jnp.float32)
-    for j in range(rows):
-        for b in energy[j]:
-            unit = jnp.where(row == j % 8, 2.0, 0.0) if b == j // 8 else 0.0
-            term = energy[j][b] * (unit - metric[j][b])
-            total = total + (term if b == j // 8 else term + term)
-    total = jnp.sum(total, axis=0, keepdims=True)
+    energy, metric = joint[:rows], joint[rows:]
+    twice = jnp.where(r[:rows, :rows] == c[:rows, :rows], 2.0, 0.0)
+    total = jnp.sum(jnp.sum(energy * (twice - metric), axis=0, keepdims=True), axis=1, keepdims=True)
     damping = 0.1 * total / rows + 1e-06 * scale
-    columns = [{b: energy[j][b] + damping * metric[j][b] for b in energy[j]} for j in range(rows)]
+    columns = spread(energy + damping * metric, rows, 2 * count)
     solved, _ = eliminate(columns, both)
     return solved[:, :count], solved[:, count:], enough
 

time: 34.4 us -> 34.5 us (level)
  no operation moved by 1% of the time
where the time goes in v16:
time: 34.5 us; the launch traced here: 34.3 us
  blocking collectives  22.2 us (64%)
  Pallas kernels  10.2 us (30%)
  local copies, waits for them, and re-layouts  1.82 us (5%)
    all_to_all x1, blocking collectives, gram_route(): lax.all_to_all(messages, ('mod', 'grp'), split_axis=0, concat_axis=0, til...  22.2 us
    pallas_call x1, Pallas kernels, gram_route(): pl.pallas_call(functools.partial(combine_kernel, rows, groups, own), out_...  9.09 us
    unnamed x6, local copies, waits for them, and re-layouts  1.62 us
    pallas_call x1, Pallas kernels, gram_route(): pl.pallas_call(features_kernel, out_shape=jax.ShapeDtypeStruct((modules,...  1.15 us

profile of v16, /device:TPU:1, one launch (start us, length us, event | category | flops | bytes accessed | tf_op | source)
XLA Modules:
  0.0 34.3 jit_solution(795164311810747399)
XLA Ops:
  0.0 0.0 copy-start.2
  0.0 0.0 copy-start.1
  0.0 0.7 %copy-done.2 = s32[8]{0:T(128)S(1)} copy-done((s32[8]{0:T(128)S(1)}, s32[8]{0:T(128)}, u32[]{:S(2)}) %copy-start.2) | copy-done | bytes 56
  0.7 0.0 copy-done.1
  0.7 0.0 copy-start
  0.7 0.9 %copy-done = bf16[2,64,8,128]{3,2,1,0:T(8,128)(2,1)S(1)} copy-done((bf16[2,64,8,128]{3,2,1,0:T(8,128)(2,1)S(1)}, bf16[2,64,8,128]{3,2,1,0:T(8,128)(2,1)}, u32[]{:S(2)}) %copy-start) | copy-done | bytes 262168
  1.6 1.1 %shard_map.37 = bf16[8,4,64,128]{3,2,1,0:T(8,128)(2,1)S(1)} custom-call(s32[2]{0:T(128)S(1)} %copy-done.1, s32[8]{0:T(128)S(1)} %copy-done.2, bf16[2,512,128]{2,1,0:T(8,128)(2,1)S(1)} %bitcast.7), custom_call_target="tpu_custom_call" | custom-call | tf_op jit(solution)/shard_map/pallas_call | solution.py:282
  2.8 22.2 %all_to_all.5 = bf16[32,2,4096]{2,1,0:T(2,128)(2,1)S(1)} all-to-all(bf16[32,2,4096]{2,1,0:T(2,128)(2,1)S(1)} %bitcast.6), channel_id=1, replica_groups=mesh['grp'=4,'mod'=8] {'mod','grp'}, dimensions={0} | all-to-all | bytes 1048576 | tf_op jit(solution)/shard_map/all_to_all | solution.py:293
  25.0 0.2 reshape.15.leaf_ref
  25.2 9.1 %shard_map.38 = f32[1,16,4096]{2,1,0:T(8,128)} custom-call(bf16[64,4096]{1,0:T(8,128)(2,1)S(1)} %reshape.15.leaf_ref), custom_call_target="tpu_custom_call" | custom-call | tf_op jit(solution)/shard_map/pallas_call | solution.py:295
Async XLA Ops:
  0.0 0.7 %copy-start.2 = (s32[8]{0:T(128)S(1)}, s32[8]{0:T(128)}, u32[]{:S(2)}) copy-start(s32[8]{0:T(128)} %order_ref.1) | copy-start | bytes 100
  0.0 0.7 %copy-start.1 = (s32[2]{0:T(128)S(1)}, s32[2]{0:T(128)}, u32[]{:S(2)}) copy-start(s32[2]{0:T(128)} %lengths_ref.1) | copy-start | bytes 28
  0.7 0.9 %copy-start = (bf16[2,64,8,128]{3,2,1,0:T(8,128)(2,1)S(1)}, bf16[2,64,8,128]{3,2,1,0:T(8,128)(2,1)}, u32[]{:S(2)}) copy-start(bf16[2,64,8,128]{3,2,1,0:T(8,128)(2,1)} %param.3) | copy-start | bytes 786436
